TPU v7x, 256 devices: a whole 4x4x8 slice. The times are simulated.
256 devices in a mesh: span: 8 (over y_lo, x), rows: 32 (over y_hi, z, core).
Axes of the slice: x: 4, y: 4 (y_hi: 2, y_lo: 2; y = y_hi * 2 + y_lo), z: 8, core: 2. Of those that a mesh axis runs over, the one named last changes fastest.
Arguments:
- queries: bfloat16 [1024, 4, 8192], P(('span', 'rows')), may hold values from -150 to 150
- prefix_keys: bfloat16 [1024, 1024], P('span'), may hold values from -6 to 6
- prefix_values: bfloat16 [1024, 1024], P('span'), may hold values from -6 to 6
- prefix_mask: int32 [1024, 8], P(('span', 'rows')), may hold values 0 or 1
- suffix_keys: bfloat16 [512, 512, 1024], P(('span', 'rows')), may hold values from -6 to 6
- suffix_values: bfloat16 [512, 512, 1024], P(('span', 'rows')), may hold values from -6 to 6
- suffix_len: int32 [512], P(('span', 'rows')), may hold values from 1 to 512, 131072 in all
- row_branch: int32 [1024], P(('span', 'rows')), may hold values from 0 to 1
- new_keys: bfloat16 [1024, 4, 1024], P(('span', 'rows')), may hold values from -6 to 6
- new_values: bfloat16 [1024, 4, 1024], P(('span', 'rows')), may hold values from -6 to 6
Outputs:
- attended: bfloat16 [1024, 4, 8192], P(('span', 'rows'))
Inputs may be any that keep to these rules, and one draw needn't show every extreme that they name: `suffix_len`: some branch uses all 512 slots.
All inputs are finite; a program needn't handle non-finite values. No bound on the sum of `prefix_mask` or of `suffix_len` on one device may be relied on, other than what follows from the above.
Results may differ from a plain program's by a relative error of at most 0.008.
Values may be sent and summed in bfloat16 or wider, within the bound.
No kernel may reach another device: no remote copies, remote signals or barrier semaphores. Data moves between devices by JAX's collectives and lax.ppermute only.
A program may use at most 64 MiB of HBM per device.

v0:
```python
import jax
import jax.numpy as jnp
from jax import lax
from jax.sharding import PartitionSpec as P

H = 64
KVH = 8
HD = 128
BLK = 128


masked_value = -1e30


def from_partner(value, axis, distance):
    mask = 2**distance
    pairs = [(source, source ^ mask) for source in range(lax.axis_size(axis))]
    return lax.ppermute(value, axis, pairs)


def summarize(scores, allowed):
    masked = jnp.where(allowed, scores, masked_value)
    largest = jnp.max(masked, axis=-1)
    weights = jnp.where(allowed, jnp.exp(masked - largest[..., None]), 0.0)
    return (largest, jnp.sum(weights, axis=-1), weights.astype(jnp.bfloat16))


def attend_shared(query_heads, key_rows, value_rows, allowed):
    key_count = key_rows.shape[0]
    key_heads = key_rows.reshape(key_count, KVH, HD)
    value_heads = value_rows.reshape(key_count, KVH, HD)
    scores = jnp.einsum(
        "rtjgd,njd->rtjgn", query_heads, key_heads, preferred_element_type=jnp.float32
    ) * HD ** (-0.5)
    largest, mass, weights = summarize(scores, allowed)
    mixed = jnp.einsum("rtjgn,njd->rtjgd", weights, value_heads, preferred_element_type=jnp.float32)
    return (largest, mass, mixed)


def combine(first, second):
    joint_max = jnp.maximum(first[0], second[0])
    first_factor = jnp.exp(first[0] - joint_max)
    second_factor = jnp.exp(second[0] - joint_max)
    mass = first[1] * first_factor + second[1] * second_factor
    mixed = first[2] * first_factor[..., None] + second[2] * second_factor[..., None]
    return (joint_max, mass, mixed)


def prefix_allowed(mask_rows, key_count):
    positions = jnp.arange(key_count, dtype=jnp.int32)
    block_onehot = (
        (positions // BLK)[None, :] == jnp.arange(mask_rows.shape[1], dtype=jnp.int32)[:, None]
    ).astype(jnp.float32)
    block_hits = jnp.dot(
        mask_rows.astype(jnp.float32), block_onehot, preferred_element_type=jnp.float32
    )
    return (block_hits > 0.5)[:, None, None, None, :]


def suffix_partial(query_heads, row_map, suffix_keys, suffix_values, suffix_lens):
    branch_count = suffix_keys.shape[0]
    slot_count = suffix_keys.shape[1]
    flat_keys = suffix_keys.reshape(branch_count * slot_count, -1)
    flat_values = suffix_values.reshape(branch_count * slot_count, -1)
    slot_ids = jnp.arange(branch_count * slot_count, dtype=jnp.int32)
    slot_branch = slot_ids // slot_count
    slot_index = slot_ids % slot_count
    slot_limit = jnp.broadcast_to(suffix_lens[:, None], (branch_count, slot_count)).reshape(-1)
    allowed = (slot_branch[None, :] == row_map[:, None]) & (slot_index < slot_limit)[None, :]
    return attend_shared(query_heads, flat_keys, flat_values, allowed[:, None, None, None, :])


def on_device(
    queries,
    prefix_keys,
    prefix_values,
    prefix_mask,
    suffix_keys,
    suffix_values,
    suffix_len,
    row_branch,
    new_keys,
    new_values,
):
    row_count = queries.shape[0]
    step_count = queries.shape[1]
    group = H // KVH
    query_heads = queries.reshape(row_count, step_count, KVH, group, HD)
    empty = (
        jnp.full((row_count, step_count, KVH, group), masked_value, jnp.float32),
        jnp.zeros((row_count, step_count, KVH, group), jnp.float32),
        jnp.zeros((row_count, step_count, KVH, group, HD), jnp.float32),
    )
    pieces = (
        lax.all_gather(prefix_keys, "span", axis=0, tiled=True),
        lax.all_gather(prefix_values, "span", axis=0, tiled=True),
    )
    allowed = prefix_allowed(prefix_mask, pieces[0].shape[0])
    prefix_part = combine(empty, attend_shared(query_heads, pieces[0], pieces[1], allowed))
    half_bit = lax.axis_size("rows").bit_length() - 2
    far_keys, far_values, far_lens = from_partner(
        (suffix_keys, suffix_values, suffix_len), "rows", half_bit
    )
    suffix_part = suffix_partial(query_heads, row_branch, far_keys, far_values, far_lens)
    new_key_heads = new_keys.reshape(row_count, step_count, KVH, HD)
    new_value_heads = new_values.reshape(row_count, step_count, KVH, HD)
    new_scores = jnp.einsum(
        "rtjgd,rsjd->rtjgs", query_heads, new_key_heads, preferred_element_type=jnp.float32
    ) * HD ** (-0.5)
    step_ids = jnp.arange(step_count, dtype=jnp.int32)
    causal = (step_ids[None, :] <= step_ids[:, None])[None, :, None, None, :]
    new_max, new_mass, new_weights = summarize(new_scores, causal)
    new_mixed = jnp.einsum(
        "rtjgs,rsjd->rtjgd", new_weights, new_value_heads, preferred_element_type=jnp.float32
    )
    merged = combine(combine(prefix_part, suffix_part), (new_max, new_mass, new_mixed))
    attended = merged[2] / merged[1][..., None]
    return attended.reshape(row_count, step_count, H * HD).astype(jnp.bfloat16)


def solution(mesh):
    return jax.shard_map(
        on_device,
        mesh=mesh,
        in_specs=(
            P(("span", "rows"), None, None),
            P("span", None),
            P("span", None),
            P(("span", "rows"), None),
            P(("span", "rows"), None, None),
            P(("span", "rows"), None, None),
            P(("span", "rows")),
            P(("span", "rows")),
            P(("span", "rows"), None, None),
            P(("span", "rows"), None, None),
        ),
        out_specs=P(("span", "rows"), None, None),
        check_vma=False,
    )
```

profile of v0, /device:TPU:1, one launch (start us, length us, event | category | flops | bytes accessed | tf_op | source)
XLA Modules:
  0.0 169.4 jit_solution(14289717802816394473)
XLA Ops:
  6.5 1.8 %copy.54 = bf16[128,1024]{0,1:T(8,128)(2,1)} copy(bf16[128,1024]{1,0:T(8,128)(2,1)} %param.11) | data formatting | bytes 524288 | tf_op args[1]
  8.3 0.0 all-gather.3.cloned.1.call-update
  8.4 0.0 all-gather.5.cloned.1.call-start
  8.4 3.8 %collective-permute-start.1 = (bf16[2,512,1024]{2,1,0:T(8,128)(2,1)}, bf16[2,512,1024]{2,1,0:T(8,128)(2,1)}, u32[]{:S(2)}, u32[]{:S(2)}) collective-permute-start(bf16[2,512,1024]{2,1,0:T(8,128)(2,1)} %param.14), channel_id=1, source_target_pairs={{0,16},{1,17},{2,18},{3,19},{4,20},{5,21},{6,22},{7,23},{8,24},{9,... | collective-permute-start | bytes 6291464 | tf_op jit(solution)/shard_map/ppermute | solution.py:18
  12.3 0.1 collective-permute-start.2
  12.4 2.9 %collective-permute-start = (s32[2]{0:T(128)}, s32[2]{0:T(128)S(1)}, u32[]{:S(2)}, u32[]{:S(2)}) collective-permute-start(s32[2]{0:T(128)} %param.16), channel_id=1, source_target_pairs={{0,16},{1,17},{2,18},{3,19},{4,20},{5,21},{6,22},{7,23},{8,24},{9,... | collective-permute-start | bytes 32 | tf_op jit(solution)/shard_map/ppermute | solution.py:18
  15.2 1.8 %copy.57 = bf16[128,1024]{0,1:T(8,128)(2,1)} copy(bf16[128,1024]{1,0:T(8,128)(2,1)} %param.12) | data formatting | bytes 524288 | tf_op args[2]
  17.0 0.0 all-gather.5.cloned.1.call-update
  17.0 1.2 reshape.172
  18.3 0.8 reshape.176
  19.1 0.8 fusion.61
  19.9 1.3 fusion.97
  21.2 0.3 fusion.67
  21.5 119.6 %collective-permute-done = s32[2]{0:T(128)S(1)} collective-permute-done((s32[2]{0:T(128)}, s32[2]{0:T(128)S(1)}, u32[]{:S(2)}, u32[]{:S(2)}) %collective-permute-start) | collective-permute-done | bytes 40 | tf_op jit(solution)/shard_map/ppermute | solution.py:18
  141.1 0.1 broadcast_bitcast_fusion
  141.2 0.7 compare_and_fusion
  141.9 0.0 collective-permute-done.1
  142.0 2.2 %copy.87 = bf16[128,8,8,128]{3,2,1,0:T(8,128)(2,1)S(1)} copy(bf16[128,8,8,128]{3,1,2,0:T(8,128)(2,1)} %bitcast.28) | data formatting | bytes 4194304
  144.2 2.0 %copy.88 = bf16[128,8,8,128]{3,2,1,0:T(8,128)(2,1)} copy(bf16[128,8,8,128]{3,1,2,0:T(8,128)(2,1)S(1)} %bitcast.107) | data formatting | bytes 4194304
  146.2 2.9 %fusion.1 = (f32[4,4,8,8]{3,1,0,2:T(4,128)S(1)}, f32[8,1024,4,4,8]{1,4,3,2,0:T(8,128)}) fusion(pred[4,1024]{1,0:T(4,128)(4,1)S(1)} %compare_and_fusion, bf16[4,4,8,8,128]{4,3,2,1,0:T(8,128)(2,1)S(1)} %reshape.172, bf16[1024,8,128,1,1]{2,1,0,4,3:T(8,128)(2,1)S(1)} %bitcast.109), kind=kOutput, calls=%fused_computation.5 | convolution fusion | flops 271580160 | bytes 6561792 | tf_op jit(solution)/shard_map/rtjgd,njd->rtjgn/dot_general | solution.py:32
  149.1 0.0 all-gather.3.cloned.1.call-done
  149.1 2.7 %fusion = (f32[4,4,8,8]{3,1,0,2:T(4,128)S(1)}, f32[8,1024,4,4,8]{1,4,3,2,0:T(8,128)S(1)}) fusion(pred[4,1024]{1,0:T(4,128)(4,1)S(1)} %fusion.61, bf16[1024,8,128,1,1]{0,2,4,3,1:T(8,128)(2,1)} %bitcast.113, bf16[4,4,8,8,128]{4,3,2,1,0:T(8,128)(2,1)S(1)} %reshape.172), kind=kOutput, calls=%fused_computation.4 | convolution fusion | flops 271580160 | bytes 6561792 | tf_op jit(solution)/shard_map/rtjgd,njd->rtjgn/dot_general | solution.py:32
  151.9 0.1 copy-done.1
  151.9 2.6 %fusion.2 = (f32[4,4,8,8]{3,1,0,2:T(4,128)S(1)}, f32[4,4,8,8]{3,1,0,2:T(4,128)S(1)}) fusion(f32[8,1024,4,4,8]{1,4,3,2,0:T(8,128)S(1)} %get-tuple-element.15, f32[4,4,8,8]{3,1,0,2:T(4,128)S(1)} %get-tuple-element.14, pred[4,1024]{1,0:T(4,128)(4,1)S(1)} %fusion.61, f32[4,4,8,8]{3,1,0,2:T(4,128)S(1)} %get-tuple-element.18, ...), kind=kLoop, calls=%fused_computation.6 | loop fusion | flops 10483712 | bytes 8413184 | tf_op jit(solution)/shard_map/reduce_sum | solution.py:25
  154.5 0.1 fusion.75
  154.6 0.0 all-gather.5.cloned.1.call-done
  154.7 4.4 %fusion.45 = f32[4,4,8,8,128]{4,3,1,0,2:T(8,128)S(1)} fusion(bf16[1024,8,128,1,1]{0,2,4,3,1:T(8,128)(2,1)} %bitcast.112, f32[8,1024,4,4,8]{1,4,3,2,0:T(8,128)} %copy-done.3, f32[4,4,8,8]{3,1,0,2:T(4,128)S(1)} %get-tuple-element.14, pred[4,1024]{1,0:T(4,128)(4,1)S(1)} %fusion.61, f32[4,4,8,8]{3,1,0,2:T(4,128)S(1)} %get-tuple-element.9, ...), kind=kOutput, calls=%fused_computation.34 | convolution fusion | flops 274071552 | bytes 6836224 | tf_op jit(solution)/shard_map/rtjgn,njd->rtjgd/dot_general | solution.py:36
  159.1 0.3 copy-done.4
  159.4 1.8 %fusion.53 = f32[4,4,8,8,128]{4,3,1,0,2:T(8,128)S(1)} fusion(f32[4,4,8,8,128]{4,3,1,0,2:T(8,128)S(1)} %fusion.45, bf16[1024,8,128,1,1]{2,1,0,4,3:T(8,128)(2,1)S(1)} %bitcast.108, f32[8,1024,4,4,8]{1,4,3,2,0:T(8,128)S(1)} %copy-done.2, f32[4,4,8,8]{3,1,0,2:T(4,128)S(1)} %get-tuple-element.18, pred[4,1024]{1,0:T(4,128)(4,1)S(1)} %compare_and_fusion, ...), kind=kOutput, calls=%fused_computation.36 | convolution fusion | flops 274071552 | bytes 7356416 | tf_op jit(solution)/shard_map/rtjgn,njd->rtjgd/dot_general | solution.py:36
  161.3 0.5 fusion.58
  161.7 0.1 copy.69
  161.8 0.8 convert_element_type.24
  (15 shorter events, 0.1 us)
Async XLA Ops:
  6.5 13.4 %copy-start = (bf16[4,4,1024]{2,1,0:T(4,128)(2,1)S(1)}, bf16[4,4,1024]{2,1,0:T(4,128)(2,1)}, u32[]{:S(2)}) copy-start(bf16[4,4,1024]{2,1,0:T(4,128)(2,1)} %param.18) | copy-start | bytes 98308
  6.5 142.6 %all-gather.3.cloned.1.call-start = ((), (), s32[]{:S(2)}) async-start(), calls=%async_computation | async-start | bytes 2359296 | tf_op jit(solution)/shard_map/all_gather | solution.py:95
  8.4 146.3 %all-gather.5.cloned.1.call-start = ((), (), s32[]{:S(2)}) async-start(), calls=%async_computation.1 | async-start | bytes 2359296 | tf_op jit(solution)/shard_map/all_gather | solution.py:96
  8.4 133.5 %collective-permute-start.1 = (bf16[2,512,1024]{2,1,0:T(8,128)(2,1)}, bf16[2,512,1024]{2,1,0:T(8,128)(2,1)}, u32[]{:S(2)}, u32[]{:S(2)}) collective-permute-start(bf16[2,512,1024]{2,1,0:T(8,128)(2,1)} %param.14), channel_id=1, source_target_pairs={{0,16},{1,17},{2,18},{3,19},{4,20},{5,21},{6,22},{7,23},{8,24},{9,... | collective-permute-start | bytes 6291464 | tf_op jit(solution)/shard_map/ppermute | solution.py:18
  12.3 131.9 %collective-permute-start.2 = (bf16[2,512,1024]{2,1,0:T(8,128)(2,1)}, bf16[2,512,1024]{2,1,0:T(8,128)(2,1)S(1)}, u32[]{:S(2)}, u32[]{:S(2)}) collective-permute-start(bf16[2,512,1024]{2,1,0:T(8,128)(2,1)} %param.15), channel_id=1, source_target_pairs={{0,16},{1,17},{2,18},{3,19},{4,20},{5,21},{6,22},{7,23},{8,24},{9,... | collective-permute-start | bytes 6291464 | tf_op jit(solution)/shard_map/ppermute | solution.py:18
  12.4 128.8 %collective-permute-start = (s32[2]{0:T(128)}, s32[2]{0:T(128)S(1)}, u32[]{:S(2)}, u32[]{:S(2)}) collective-permute-start(s32[2]{0:T(128)} %param.16), channel_id=1, source_target_pairs={{0,16},{1,17},{2,18},{3,19},{4,20},{5,21},{6,22},{7,23},{8,24},{9,... | collective-permute-start | bytes 32 | tf_op jit(solution)/shard_map/ppermute | solution.py:18
  149.1 2.8 %copy-start.1 = (f32[8,1024,4,4,8]{1,4,3,2,0:T(8,128)S(1)}, f32[8,1024,4,4,8]{1,4,3,2,0:T(8,128)}, u32[]{:S(2)}) copy-start(f32[8,1024,4,4,8]{1,4,3,2,0:T(8,128)} %get-tuple-element.19) | copy-start | bytes 12582916
  151.9 2.6 %copy-start.3 = (f32[8,1024,4,4,8]{1,4,3,2,0:T(8,128)}, f32[8,1024,4,4,8]{1,4,3,2,0:T(8,128)S(1)}, u32[]{:S(2)}) copy-start(f32[8,1024,4,4,8]{1,4,3,2,0:T(8,128)S(1)} %get-tuple-element.15) | copy-start | bytes 12582916
  154.7 4.4 %copy-start.2 = (f32[8,1024,4,4,8]{1,4,3,2,0:T(8,128)S(1)}, f32[8,1024,4,4,8]{1,4,3,2,0:T(8,128)}, u32[]{:S(2)}) copy-start(f32[8,1024,4,4,8]{1,4,3,2,0:T(8,128)} %get-tuple-element.19) | copy-start | bytes 12582916
  154.7 4.7 %copy-start.4 = (bf16[128,8,8,128]{3,2,1,0:T(8,128)(2,1)S(1)}, bf16[128,8,8,128]{3,2,1,0:T(8,128)(2,1)}, u32[]{:S(2)}) copy-start(bf16[128,8,8,128]{3,2,1,0:T(8,128)(2,1)} %copy.88) | copy-start | bytes 6291460
Sparse Core Ops, SparseCore 0:
  9.1 47.6 all-gather.2
  58.5 48.1 all-gather.4
where the time goes:
time: 171 us; the launch traced here: 169 us
  waiting for transfers between devices  120 us (70%)
  matrix products  14.4 us (8%)
  between operations  13.6 us (8%)
  local copies, waits for them, and re-layouts  11.1 us (6%)
  starting transfers between devices  6.84 us (4%)
  other arithmetic  3.78 us (2%)
    ppermute x3, waiting for transfers between devices, from_partner(): return lax.ppermute(value, axis, pairs)  120 us
    unnamed x16, local copies, waits for them, and re-layouts  8.26 us
    ppermute x3, starting transfers between devices, from_partner(): return lax.ppermute(value, axis, pairs)  6.8 us
    dot_general x2, matrix products, attend_shared(): jnp.einsum('rtjgn,njd->rtjgd', weights, value_heads, preferred_element_ty...  6.24 us
    dot_general x2, matrix products, attend_shared(): jnp.einsum('rtjgd,njd->rtjgn', query_heads, key_heads, preferred_element_...  5.63 us
  transfers between devices with their start and end apart: 5, of which 1 were waited for; matrix products, arithmetic and copies ran while one was open for 12% of the time, Pallas kernels for 0%

commit v1 on v0

v1 whole, which is shorter than its diff:
```python
import functools

import jax
import jax.numpy as jnp
from jax import lax
from jax.experimental import pallas as pl
from jax.experimental.pallas import tpu as pltpu
from jax.sharding import PartitionSpec as P

H = 64
KVH = 8
HD = 128
GROUP = H // KVH
AXES = ("span", "rows")
MASKED = -1e30
SCALE = 1.4426950408889634 * HD ** (-0.5)
ROWS = 4
STEPS = 4
QR = GROUP * STEPS
NQ = ROWS * QR
TOTAL = KVH * NQ
EXT = 16
STAT = 32


def device_id(x, y, z, c):
    x, y, z, c = x % 4, y % 4, z % 8, c % 2
    return ((y % 2) * 4 + x) * 32 + (y // 2) * 16 + z * 2 + c


def send(value, target):
    pairs = [
        (device_id(x, y, z, c), device_id(*target(x, y, z, c)))
        for x in range(4)
        for y in range(4)
        for z in range(8)
        for c in range(2)
    ]
    return lax.ppermute(value, AXES, pairs)


def to_partner(x, y, z, c):
    return (x, y + 2, z, c)


def to_neighbour(x, y, z, c):
    return (x, y + 1 - 2 * c, z, c)


def from_neighbour(x, y, z, c):
    return (x, y - 1 + 2 * c, z, c)


def along_x(x, y, z, c):
    return (x + 1 - 2 * c, y, z, c)


def across_x(x, y, z, c):
    return (x + 2, y, z, c)


def other_core(x, y, z, c):
    return (x, y, z, 1 - c)


def dot_nt(a, b):
    return lax.dot_general(a, b, (((1,), (1,)), ((), ())), preferred_element_type=jnp.float32)


def dot_nn(a, b):
    return lax.dot_general(a, b, (((1,), (0,)), ((), ())), preferred_element_type=jnp.float32)


def head_rows(ref, j):
    return jnp.concatenate([ref[r * 256 + j * QR : r * 256 + (j + 1) * QR, :] for r in range(ROWS)], axis=0)


def ext_column(q_ref, lane):
    ext = q_ref[TOTAL : TOTAL + ROWS * EXT, :].astype(jnp.float32)
    lanes = lax.broadcasted_iota(jnp.int32, ext.shape, 1)
    column = jnp.sum(jnp.where(lanes == lane, ext, 0.0), axis=1, keepdims=True)
    pieces = []
    for r in range(ROWS):
        piece = column[r * EXT : (r + 1) * EXT, :]
        pieces += [piece, piece]
    return jnp.concatenate(pieces, axis=0)


def pack_stats(stat):
    rows = stat.T[:KVH, :]
    hi = rows.astype(jnp.bfloat16)
    rest = rows - hi.astype(jnp.float32)
    mid = rest.astype(jnp.bfloat16)
    low = (rest - mid.astype(jnp.float32)).astype(jnp.bfloat16)
    pad = jnp.zeros_like(hi)
    return jnp.concatenate([hi, mid, low, pad], axis=0)


def unpack_stats(ref):
    rows = ref[TOTAL : TOTAL + STAT, :].astype(jnp.float32)
    rows = rows[:KVH] + rows[KVH : 2 * KVH] + rows[2 * KVH : 3 * KVH]
    full = jnp.concatenate([rows, jnp.zeros((NQ - KVH, NQ), jnp.float32)], axis=0)
    return full.T


def suffix_kernel(len_ref, q_ref, k_hbm, v_hbm, out_ref, k_buf, v_buf, sems):
    def copies(j):
        cols = slice(j * HD, (j + 1) * HD)
        return (
            pltpu.make_async_copy(k_hbm.at[:, :, cols], k_buf.at[:, :, cols], sems.at[0, j]),
            pltpu.make_async_copy(v_hbm.at[:, :, cols], v_buf.at[:, :, cols], sems.at[1, j]),
        )

    for j in range(KVH):
        for copy in copies(j):
            copy.start()
    slots = k_buf.shape[1]
    second = ext_column(q_ref, KVH) > 0.5
    length = jnp.where(second, len_ref[1], len_ref[0])
    allowed = lax.broadcasted_iota(jnp.int32, (NQ, slots), 1) < length
    lanes = lax.broadcasted_iota(jnp.int32, (NQ, 128), 1)
    stat = jnp.zeros((NQ, 128), jnp.float32)
    for j in range(KVH):
        cols = slice(j * HD, (j + 1) * HD)
        query = head_rows(q_ref, j)
        for copy in copies(j):
            copy.wait()
        scores = jnp.where(second, dot_nt(query, k_buf[1, :, cols]), dot_nt(query, k_buf[0, :, cols]))
        scores = jnp.where(allowed, scores, MASKED)
        largest = jnp.max(scores, axis=1, keepdims=True)
        weights = jnp.exp2((scores - largest) * SCALE)
        mass = jnp.sum(weights, axis=1, keepdims=True)
        rounded = weights.astype(jnp.bfloat16)
        mixed = jnp.where(second, dot_nn(rounded, v_buf[1, :, cols]), dot_nn(rounded, v_buf[0, :, cols]))
        result = (mixed / mass).astype(jnp.bfloat16)
        for r in range(ROWS):
            out_ref[r * 256 + j * QR : r * 256 + (j + 1) * QR, :] = result[r * QR : (r + 1) * QR, :]
        stat = jnp.where(lanes == j, largest * SCALE + jnp.log2(mass), stat)
    out_ref[TOTAL : TOTAL + STAT, :] = pack_stats(stat)


def gather_blocks(refs, k_buf, v_buf, sems, core):
    k_own, v_own, kv_near, kv_far, half_own, half_other = refs
    pairs = [
        (k_own, k_buf.at[0]),
        (v_own, v_buf.at[0]),
        (kv_near.at[0], k_buf.at[1]),
        (kv_near.at[1], v_buf.at[1]),
        (kv_far.at[0], k_buf.at[2]),
        (kv_far.at[1], v_buf.at[2]),
    ]
    copies = [pltpu.make_async_copy(a, b, sems.at[i]) for i, (a, b) in enumerate(pairs)]
    for copy in copies:
        copy.start()

    def halves(k_half, v_half):
        return (
            pltpu.make_async_copy(k_half, k_buf.at[3], sems.at[6]),
            pltpu.make_async_copy(v_half, v_buf.at[3], sems.at[7]),
        )

    @pl.when(core == 0)
    def _():
        for copy in halves(half_own, half_other):
            copy.start()

    @pl.when(core == 1)
    def _():
        for copy in halves(half_other, half_own):
            copy.start()

    for copy in copies:
        copy.wait()
    for copy in halves(half_own, half_other):
        copy.wait()


def prefix_kernel(with_new, *refs):
    if with_new:
        (q_ref, k_own, v_own, kv_near, kv_far, half_own, half_other, nk_ref, nv_ref, out_ref, stat_ref, k_buf, v_buf, sems) = refs
    else:
        (q_ref, k_own, v_own, kv_near, kv_far, half_own, half_other, out_ref, k_buf, v_buf, sems) = refs
    span = lax.axis_index("span")
    core = lax.rem(lax.axis_index("rows"), 2)
    x = lax.rem(span, 4)
    first = span - x
    gather_blocks((k_own, v_own, kv_near, kv_far, half_own, half_other), k_buf, v_buf, sems, core)
    offsets = (0, 3 + 2 * core, 5 - 2 * core, 2)
    allowed = [ext_column(q_ref, first + lax.rem(x + offset, 4)) > 0.5 for offset in offsets]
    lanes = lax.broadcasted_iota(jnp.int32, (NQ, 128), 1)
    stat = jnp.zeros((NQ, 128), jnp.float32)
    if with_new:
        row_of = lax.broadcasted_iota(jnp.int32, (NQ, 128), 0)
        same_row = (row_of // QR) == (lanes // (KVH * STEPS))
        causal = (lanes % STEPS) <= (row_of % STEPS)
        new_base = same_row & causal
        new_head = (lanes // STEPS) % KVH
    for j in range(KVH):
        cols = slice(j * HD, (j + 1) * HD)
        query = head_rows(q_ref, j)
        parts = []
        for i in range(4):
            scores = dot_nt(query, k_buf[i, :, cols])
            parts.append(jnp.where(allowed[i], scores, MASKED))
        if with_new:
            parts.append(jnp.where(new_base & (new_head == j), dot_nt(query, nk_ref[...]), MASKED))
        largest = functools.reduce(jnp.maximum, parts)
        largest = jnp.max(largest, axis=1, keepdims=True)
        weights = [jnp.exp2((part - largest) * SCALE) for part in parts]
        mass = jnp.sum(functools.reduce(jnp.add, weights), axis=1, keepdims=True)
        mixed = functools.reduce(
            jnp.add, [dot_nn(weights[i].astype(jnp.bfloat16), v_buf[i, :, cols]) for i in range(4)]
        )
        if with_new:
            mixed = mixed + dot_nn(weights[4].astype(jnp.bfloat16), nv_ref[...])
        result = (mixed / mass).astype(out_ref.dtype)
        for r in range(ROWS):
            out_ref[r * 256 + j * QR : r * 256 + (j + 1) * QR, :] = result[r * QR : (r + 1) * QR, :]
        stat = jnp.where(lanes == j, largest * SCALE + jnp.log2(mass), stat)
    if with_new:
        stat_ref[...] = stat
    else:
        out_ref[TOTAL : TOTAL + STAT, :] = pack_stats(stat)


def combine_kernel(own_ref, stat_ref, far_ref, near_ref, out_ref):
    own, far, near = stat_ref[...], unpack_stats(far_ref), unpack_stats(near_ref)
    top = jnp.maximum(jnp.maximum(own, far), near)
    own, far, near = jnp.exp2(own - top), jnp.exp2(far - top), jnp.exp2(near - top)
    scale = 1.0 / (own + far + near)
    own, far, near = own * scale, far * scale, near * scale
    for j in range(KVH):
        for r in range(ROWS):
            rows = slice(r * 256 + j * QR, r * 256 + (j + 1) * QR)
            part = slice(r * QR, (r + 1) * QR)
            out_ref[rows, :] = (
                own_ref[rows, :] * own[part, j : j + 1]
                + far_ref[rows, :].astype(jnp.float32) * far[part, j : j + 1]
                + near_ref[rows, :].astype(jnp.float32) * near[part, j : j + 1]
            ).astype(jnp.bfloat16)


VMEM = pl.BlockSpec(memory_space=pltpu.VMEM)
SMEM = pl.BlockSpec(memory_space=pltpu.SMEM)
ANY = pl.BlockSpec(memory_space=pl.ANY)
PACKED = jax.ShapeDtypeStruct((TOTAL + STAT, HD), jnp.bfloat16)


def call(kernel, args, specs, out, scratch, flops):
    return pl.pallas_call(
        kernel,
        out_shape=out,
        in_specs=specs,
        out_specs=jax.tree.map(lambda _: VMEM, out),
        scratch_shapes=scratch,
        cost_estimate=pl.CostEstimate(flops=flops, bytes_accessed=4 << 20, transcendentals=1 << 19),
        compiler_params=pltpu.CompilerParams(vmem_limit_bytes=32 << 20),
    )(*args)


def heads_first(value, heads):
    rows, steps, _ = value.shape
    return value.reshape(rows, steps, heads, HD).transpose(0, 2, 1, 3).reshape(rows * heads * steps, HD)


def on_device(
    queries,
    prefix_keys,
    prefix_values,
    prefix_mask,
    suffix_keys,
    suffix_values,
    suffix_len,
    row_branch,
    new_keys,
    new_values,
):
    core = lax.rem(lax.axis_index("rows"), 2)
    extra = jnp.concatenate([prefix_mask, row_branch[:, None]], axis=1).astype(jnp.bfloat16)
    extra = jnp.pad(extra, ((0, 0), (0, HD - extra.shape[1])))
    extra = jnp.broadcast_to(extra[:, None, :], (ROWS, EXT, HD)).reshape(ROWS * EXT, HD)
    packed = jnp.concatenate([heads_first(queries, H), extra], axis=0)
    far_queries = send(packed, to_partner)
    near_queries = send(packed, to_neighbour)
    both = jnp.stack([prefix_keys, prefix_values])
    kv_near = send(both, along_x)
    half_own = send(lax.dynamic_index_in_dim(both, core, 0, keepdims=False), across_x)
    kv_far = send(kv_near, other_core)
    half_other = send(half_own, other_core)

    suffix = call(
        suffix_kernel,
        (suffix_len, far_queries, suffix_keys, suffix_values),
        [SMEM, VMEM, ANY, ANY],
        PACKED,
        [
            pltpu.VMEM(suffix_keys.shape, jnp.bfloat16),
            pltpu.VMEM(suffix_values.shape, jnp.bfloat16),
            pltpu.SemaphoreType.DMA((2, KVH)),
        ],
        2 << 28,
    )
    suffix = send(suffix, to_partner)

    blocks = (prefix_keys, prefix_values, kv_near, kv_far, half_own, half_other)
    scratch = [
        pltpu.VMEM((4,) + prefix_keys.shape, jnp.bfloat16),
        pltpu.VMEM((4,) + prefix_values.shape, jnp.bfloat16),
        pltpu.SemaphoreType.DMA((8,)),
    ]
    near = call(
        functools.partial(prefix_kernel, False),
        (near_queries,) + blocks,
        [VMEM] + [ANY] * 6,
        PACKED,
        scratch,
        1 << 28,
    )
    near = send(near, from_neighbour)
    own, stat = call(
        functools.partial(prefix_kernel, True),
        (packed,) + blocks + (heads_first(new_keys, KVH), heads_first(new_values, KVH)),
        [VMEM] + [ANY] * 6 + [VMEM] * 2,
        (jax.ShapeDtypeStruct((TOTAL, HD), jnp.float32), jax.ShapeDtypeStruct((NQ, 128), jnp.float32)),
        scratch,
        1 << 28,
    )
    merged = call(
        combine_kernel,
        (own, stat, suffix, near),
        [VMEM] * 4,
        jax.ShapeDtypeStruct((TOTAL, HD), jnp.bfloat16),
        [],
        1 << 20,
    )
    merged = merged.reshape(ROWS, H, STEPS, HD).transpose(0, 2, 1, 3)
    return merged.reshape(queries.shape)


def solution(mesh):
    return jax.shard_map(
        on_device,
        mesh=mesh,
        in_specs=(
            P(AXES, None, None),
            P("span", None),
            P("span", None),
            P(AXES, None),
            P(AXES, None, None),
            P(AXES, None, None),
            P(AXES),
            P(AXES),
            P(AXES, None, None),
            P(AXES, None, None),
        ),
        out_specs=P(AXES, None, None),
        check_vma=False,
    )
```

time: 171 us -> 53.4 us (0.31)
  waiting for transfers between devices: 120 us -> 23.1 us
  matrix products: 14.4 us -> 0 us
  Pallas kernels: 0 us -> 14 us
  between operations: 13.6 us -> 0.15 us
  local copies, waits for them, and re-layouts: 11.1 us -> 1.74 us
  starting transfers between devices: 6.84 us -> 8.75 us
    ppermute x3 -> x8, waiting for transfers between devices: 120 us -> 23.1 us  [send(): return lax.ppermute(value, AXES, pairs)]
    dot_general x7 -> x0, matrix products: 14.4 us -> none  [the longest x2 6.24 us: attend_shared(): jnp.einsum('rtjgn,njd->rtjgd', weights, value_heads, preferred_element_ty...]
    pallas_call x0 -> x4, Pallas kernels: none -> 14 us  [call(): pl.pallas_call(kernel, out_shape=out, in_specs=specs, out_specs=jax.tree....]
    unnamed x16 -> x14, local copies, waits for them, and re-layouts: 8.26 us -> 1.62 us
    reduce_sum x1 -> x0, other arithmetic: 2.55 us -> none  [summarize(): return (largest, jnp.sum(weights, axis=-1), weights.astype(jnp.bfloat16))]
    reshape x2 -> x0, local copies, waits for them, and re-layouts: 2.01 us -> none  [the longest x1 1.23 us: on_device(): query_heads = queries.reshape(row_count, step_count, KVH, group, HD)]
    ppermute x3 -> x8, starting transfers between devices: 6.8 us -> 8.75 us  [send(): return lax.ppermute(value, AXES, pairs)]
    another operation x0 -> x2, other arithmetic: none -> 1.91 us  [the longest x1 1.23 us: on_device(): both = jnp.stack([prefix_keys, prefix_values])]
  transfers between devices with their start and end apart: 5 -> 8, of which waited for: 1 -> 4; matrix products, arithmetic and copies ran while one was open for 12% -> 8% of each run, Pallas kernels for 0% -> 24%
where the time goes in v1:
time: 53.4 us; the launch traced here: 53.2 us
  waiting for transfers between devices  23.1 us (43%)
  Pallas kernels  14 us (26%)
  starting transfers between devices  8.75 us (16%)
  other arithmetic  5.36 us (10%)
  local copies, waits for them, and re-layouts  1.74 us (3%)
    ppermute x8, waiting for transfers between devices, send(): return lax.ppermute(value, AXES, pairs)  23.1 us
    pallas_call x4, Pallas kernels, call(): pl.pallas_call(kernel, out_shape=out, in_specs=specs, out_specs=jax.tree....  14 us
    ppermute x8, starting transfers between devices, send(): return lax.ppermute(value, AXES, pairs)  8.75 us
    squeeze x1, other arithmetic, on_device(): lax.dynamic_index_in_dim(both, core, 0, keepdims=False)  1.75 us
    unnamed x14, local copies, waits for them, and re-layouts  1.62 us
    another operation x1, other arithmetic, on_device(): both = jnp.stack([prefix_keys, prefix_values])  1.23 us
  transfers between devices with their start and end apart: 8, of which 4 were waited for; matrix products, arithmetic and copies ran while one was open for 8% of the time, Pallas kernels for 24%

profile of v1, /device:TPU:1, one launch (start us, length us, event | category | flops | bytes accessed | tf_op | source)
XLA Modules:
  0.0 53.2 jit_solution(708847859672137829)
XLA Ops:
  0.0 1.2 %pad_maximum_fusion = bf16[2,128,1024]{2,1,0:T(8,128)(2,1)S(1)} fusion(bf16[1,128,1024]{2,1,0:T(8,128)(2,1)} %bitcast.29, bf16[1,128,1024]{2,1,0:T(8,128)(2,1)} %bitcast.27), kind=kLoop, calls=%fused_computation.1 | loop fusion | flops 262144 | bytes 1048576 | tf_op jit(solution)/shard_map/stack | solution.py:285
  1.2 3.4 %collective-permute-start = (bf16[2,128,1024]{2,1,0:T(8,128)(2,1)S(1)}, bf16[2,128,1024]{2,1,0:T(8,128)(2,1)S(1)}, u32[]{:S(2)}, u32[]{:S(2)}) collective-permute-start(bf16[2,128,1024]{2,1,0:T(8,128)(2,1)S(1)} %pad_maximum_fusion), channel_id=1, source_target_pairs={{0,32},{1,97},{2,34},{3,99},{4,36},{5,101},{6,38},{7,103},{8,40},{... | collective-permute-start | bytes 1572872 | tf_op jit(solution)/shard_map/ppermute | solution.py:39
  4.6 1.7 %fusion.1 = bf16[128,1024]{1,0:T(8,128)(2,1)} fusion(s32[]{:T(128)S(6)} %select_n.4, bf16[1,128,1024]{2,1,0:T(8,128)(2,1)} %bitcast.28, bf16[1,128,1024]{2,1,0:T(8,128)(2,1)} %bitcast.30), kind=kLoop, calls=%fused_computation.5 | loop fusion | flops 131072 | bytes 786436 | tf_op jit(solution)/shard_map/jit(dynamic_index_in_dim)/squeeze | solution.py:287
  6.4 0.5 collective-permute-start.2
  6.9 0.7 %convert_bitcast_fusion = bf16[4,1]{0,1:T(2,128)(2,1)S(1)} fusion(s32[4]{0:T(128)} %param.17), kind=kLoop, calls=%fused_computation.10 | loop fusion | flops 4 | bytes 24 | tf_op jit(solution)/shard_map/broadcast_in_dim | solution.py:279
  7.5 0.1 copy.12
  7.7 0.7 %convert.7 = bf16[4,8]{1,0:T(4,128)(2,1)S(1)} convert(s32[4,8]{1,0:T(4,128)} %param.13) | non-fusion elementwise | flops 32 | bytes 192 | tf_op jit(solution)/shard_map/convert
  8.3 0.1 fusion.4
  8.4 7.9 %collective-permute-done.refs_3_ = bf16[2,128,1024]{2,1,0:T(8,128)(2,1)S(1)} collective-permute-done((bf16[2,128,1024]{2,1,0:T(8,128)(2,1)S(1)}, bf16[2,128,1024]{2,1,0:T(8,128)(2,1)S(1)}, u32[]{:S(2)}, u32[]{:S(2)}) %collective-permute-start) | collective-permute-done | bytes 524320 | tf_op jit(solution)/shard_map/ppermute | solution.py:39
  16.4 4.2 %collective-permute-start.1 = (bf16[2,128,1024]{2,1,0:T(8,128)(2,1)S(1)}, bf16[2,128,1024]{2,1,0:T(8,128)(2,1)S(1)}, u32[]{:S(2)}, u32[]{:S(2)}) collective-permute-start(bf16[2,128,1024]{2,1,0:T(8,128)(2,1)S(1)} %collective-permute-done.refs_3_), channel_id=1, source_target_pairs={{0,1},{1,0},{2,3},{3,2},{4,5},{5,4},{6,7},{7,6},{8,9},{9,8},{10,11... | collective-permute-start | bytes 1572872 | tf_op jit(solution)/shard_map/ppermute | solution.py:39
  20.6 1.0 %pad_maximum_fusion.1.refs_0_ = bf16[1088,128]{1,0:T(8,128)(2,1)S(1)} fusion(bf16[64,128]{1,0:T(8,128)(2,1)S(1)} %bitcast.34, bf16[1024,128]{1,0:T(8,128)(2,1)} %bitcast.33), kind=kLoop, calls=%fused_computation.3 | loop fusion | flops 557056 | bytes 557056 | tf_op jit(solution)/shard_map/concatenate | solution.py:282
  21.5 0.0 copy-start
  21.6 0.0 copy-start.1
  21.6 0.1 collective-permute-start.4
  21.7 0.1 collective-permute-start.6
  21.8 0.0 collective-permute-done.2.refs_5_
  21.8 0.1 collective-permute-start.3
  21.9 9.6 %collective-permute-done.4.q_ref = bf16[1088,128]{1,0:T(8,128)(2,1)S(1)} collective-permute-done((bf16[1088,128]{1,0:T(8,128)(2,1)S(1)}, bf16[1088,128]{1,0:T(8,128)(2,1)S(1)}, u32[]{:S(2)}, u32[]{:S(2)}) %collective-permute-start.4) | collective-permute-done | bytes 278560 | tf_op jit(solution)/shard_map/ppermute | solution.py:39
  31.5 1.6 %copy-done.3 = bf16[2,512,1024]{2,1,0:T(8,128)(2,1)S(1)} copy-done((bf16[2,512,1024]{2,1,0:T(8,128)(2,1)S(1)}, bf16[2,512,1024]{2,1,0:T(8,128)(2,1)}, u32[]{:S(2)}) %copy-start.3) | copy-done | bytes 2097176
  33.1 6.0 %shard_map.101 = bf16[1056,128]{1,0:T(8,128)(2,1)S(1)} custom-call(s32[2]{0:T(128)S(1)} %copy-done.6, bf16[1088,128]{1,0:T(8,128)(2,1)S(1)} %collective-permute-done.4.q_ref, bf16[2,512,1024]{2,1,0:T(8,128)(2,1)S(1)} %copy-done.2, bf16[2,512,1024]{2,1,0:T(8,128)(2,1)S(1)} %copy-done.3), custom_call_target="tpu_custom_call" | custom-call | flops 536870912 | bytes 4194304 | tf_op jit(solution)/shard_map/pallas_call | solution.py:250
  39.1 0.0 copy-start.4
  39.1 0.0 copy-start.5
  39.1 0.3 collective-permute-start.5
  39.4 0.0 collective-permute-done.6.refs_0_
  39.4 0.0 collective-permute-done.3.refs_6_
  39.4 0.0 collective-permute-done.1.refs_4_
  39.4 3.1 %shard_map.102 = bf16[1056,128]{1,0:T(8,128)(2,1)S(1)} custom-call(bf16[1088,128]{1,0:T(8,128)(2,1)S(1)} %collective-permute-done.6.refs_0_, bf16[128,1024]{1,0:T(8,128)(2,1)S(1)} %copy-done, bf16[128,1024]{1,0:T(8,128)(2,1)S(1)} %copy-done.1, bf16[2,128,1024]{2,1,0:T(8,128)(2,1)S(1)} %collective-permute-done.refs_3_, ...), custom_call_target="tpu_custom_call" | custom-call | flops 268435456 | bytes 4194304 | tf_op jit(solution)/shard_map/pallas_call | solution.py:250
  42.5 0.1 collective-permute-start.7
  42.6 3.6 %shard_map.100 = (f32[1024,128]{1,0:T(8,128)S(1)}, f32[128,128]{1,0:T(8,128)S(1)}) custom-call(bf16[1088,128]{1,0:T(8,128)(2,1)S(1)} %pad_maximum_fusion.1.refs_0_, bf16[128,1024]{1,0:T(8,128)(2,1)S(1)} %copy-done, bf16[128,1024]{1,0:T(8,128)(2,1)S(1)} %copy-done.1, bf16[2,128,1024]{2,1,0:T(8,128)(2,1)S(1)} %collective-permute-done.refs_3_, ...), custom_call_target="tpu_custom_call" | custom-call | flops 268435456 | bytes 4194304 | tf_op jit(solution)/shard_map/pallas_call | solution.py:250
  46.2 1.6 %collective-permute-done.5.far_ref = bf16[1056,128]{1,0:T(8,128)(2,1)S(1)} collective-permute-done((bf16[1056,128]{1,0:T(8,128)(2,1)S(1)}, bf16[1056,128]{1,0:T(8,128)(2,1)S(1)}, u32[]{:S(2)}, u32[]{:S(2)}) %collective-permute-start.5) | collective-permute-done | bytes 270368 | tf_op jit(solution)/shard_map/ppermute | solution.py:39
  47.8 4.0 %collective-permute-done.7.near_ref = bf16[1056,128]{1,0:T(8,128)(2,1)S(1)} collective-permute-done((bf16[1056,128]{1,0:T(8,128)(2,1)S(1)}, bf16[1056,128]{1,0:T(8,128)(2,1)S(1)}, u32[]{:S(2)}, u32[]{:S(2)}) %collective-permute-start.7) | collective-permute-done | bytes 270368 | tf_op jit(solution)/shard_map/ppermute | solution.py:39
  51.8 1.4 %shard_map.103 = bf16[1024,128]{1,0:T(8,128)(2,1)} custom-call(f32[1024,128]{1,0:T(8,128)S(1)} %get-tuple-element.7.own_ref, f32[128,128]{1,0:T(8,128)S(1)} %get-tuple-element.8.stat_ref, bf16[1056,128]{1,0:T(8,128)(2,1)S(1)} %collective-permute-done.5.far_ref, bf16[1056,128]{1,0:T(8,128)(2,1)S(1)} %collective-permute-done.7.near_ref), custom_call_target="tpu_custom_call" | custom-call | flops 1048576 | bytes 4194304 | tf_op jit(solution)/shard_map/pallas_call | solution.py:250
  (10 shorter events, 0.0 us)
Async XLA Ops:
  0.0 31.5 %copy-start.2 = (bf16[2,512,1024]{2,1,0:T(8,128)(2,1)S(1)}, bf16[2,512,1024]{2,1,0:T(8,128)(2,1)}, u32[]{:S(2)}) copy-start(bf16[2,512,1024]{2,1,0:T(8,128)(2,1)} %k_hbm.1) | copy-start | bytes 6291460
  0.0 31.5 %copy-start.6 = (s32[2]{0:T(128)S(1)}, s32[2]{0:T(128)}, u32[]{:S(2)}) copy-start(s32[2]{0:T(128)} %len_ref.1) | copy-start | bytes 28
  1.2 15.1 %collective-permute-start = (bf16[2,128,1024]{2,1,0:T(8,128)(2,1)S(1)}, bf16[2,128,1024]{2,1,0:T(8,128)(2,1)S(1)}, u32[]{:S(2)}, u32[]{:S(2)}) collective-permute-start(bf16[2,128,1024]{2,1,0:T(8,128)(2,1)S(1)} %pad_maximum_fusion), channel_id=1, source_target_pairs={{0,32},{1,97},{2,34},{3,99},{4,36},{5,101},{6,38},{7,103},{8,40},{... | collective-permute-start | bytes 1572872 | tf_op jit(solution)/shard_map/ppermute | solution.py:39
  6.4 15.4 %collective-permute-start.2 = (bf16[128,1024]{1,0:T(8,128)(2,1)}, bf16[128,1024]{1,0:T(8,128)(2,1)S(1)}, u32[]{:S(2)}, u32[]{:S(2)}) collective-permute-start(bf16[128,1024]{1,0:T(8,128)(2,1)} %fusion.1), channel_id=1, source_target_pairs={{0,64},{1,65},{2,66},{3,67},{4,68},{5,69},{6,70},{7,71},{8,72},{9,... | collective-permute-start | bytes 786440 | tf_op jit(solution)/shard_map/ppermute | solution.py:39
  16.4 23.0 %collective-permute-start.1 = (bf16[2,128,1024]{2,1,0:T(8,128)(2,1)S(1)}, bf16[2,128,1024]{2,1,0:T(8,128)(2,1)S(1)}, u32[]{:S(2)}, u32[]{:S(2)}) collective-permute-start(bf16[2,128,1024]{2,1,0:T(8,128)(2,1)S(1)} %collective-permute-done.refs_3_), channel_id=1, source_target_pairs={{0,1},{1,0},{2,3},{3,2},{4,5},{5,4},{6,7},{7,6},{8,9},{9,8},{10,11... | collective-permute-start | bytes 1572872 | tf_op jit(solution)/shard_map/ppermute | solution.py:39
  21.5 17.9 %copy-start = (bf16[128,1024]{1,0:T(8,128)(2,1)S(1)}, bf16[128,1024]{1,0:T(8,128)(2,1)}, u32[]{:S(2)}) copy-start(bf16[128,1024]{1,0:T(8,128)(2,1)} %refs_1_.3) | copy-start | bytes 786436
  21.6 17.9 %copy-start.1 = (bf16[128,1024]{1,0:T(8,128)(2,1)S(1)}, bf16[128,1024]{1,0:T(8,128)(2,1)}, u32[]{:S(2)}) copy-start(bf16[128,1024]{1,0:T(8,128)(2,1)} %refs_2_.3) | copy-start | bytes 786436
  21.6 9.9 %collective-permute-start.4 = (bf16[1088,128]{1,0:T(8,128)(2,1)S(1)}, bf16[1088,128]{1,0:T(8,128)(2,1)S(1)}, u32[]{:S(2)}, u32[]{:S(2)}) collective-permute-start(bf16[1088,128]{1,0:T(8,128)(2,1)S(1)} %pad_maximum_fusion.1.refs_0_), channel_id=1, source_target_pairs={{0,16},{1,17},{2,18},{3,19},{4,20},{5,21},{6,22},{7,23},{8,24},{9,... | collective-permute-start | bytes 835592 | tf_op jit(solution)/shard_map/ppermute | solution.py:39
  21.7 17.7 %collective-permute-start.6 = (bf16[1088,128]{1,0:T(8,128)(2,1)S(1)}, bf16[1088,128]{1,0:T(8,128)(2,1)S(1)}, u32[]{:S(2)}, u32[]{:S(2)}) collective-permute-start(bf16[1088,128]{1,0:T(8,128)(2,1)S(1)} %pad_maximum_fusion.1.refs_0_), channel_id=1, source_target_pairs={{0,128},{1,145},{2,130},{3,147},{4,132},{5,149},{6,134},{7,151},{8... | collective-permute-start | bytes 835592 | tf_op jit(solution)/shard_map/ppermute | solution.py:39
  21.8 17.6 %collective-permute-start.3 = (bf16[128,1024]{1,0:T(8,128)(2,1)S(1)}, bf16[128,1024]{1,0:T(8,128)(2,1)S(1)}, u32[]{:S(2)}, u32[]{:S(2)}) collective-permute-start(bf16[128,1024]{1,0:T(8,128)(2,1)S(1)} %collective-permute-done.2.refs_5_), channel_id=1, source_target_pairs={{0,1},{1,0},{2,3},{3,2},{4,5},{5,4},{6,7},{7,6},{8,9},{9,8},{10,11... | collective-permute-start | bytes 786440 | tf_op jit(solution)/shard_map/ppermute | solution.py:39
  31.5 1.6 %copy-start.3 = (bf16[2,512,1024]{2,1,0:T(8,128)(2,1)S(1)}, bf16[2,512,1024]{2,1,0:T(8,128)(2,1)}, u32[]{:S(2)}) copy-start(bf16[2,512,1024]{2,1,0:T(8,128)(2,1)} %v_hbm.1) | copy-start | bytes 6291460
  39.1 3.5 %copy-start.4 = (bf16[4,4,1024]{2,1,0:T(4,128)(2,1)S(1)}, bf16[4,4,1024]{2,1,0:T(4,128)(2,1)}, u32[]{:S(2)}) copy-start(bf16[4,4,1024]{2,1,0:T(4,128)(2,1)} %param.18) | copy-start | bytes 98308
  39.1 3.5 %copy-start.5 = (bf16[4,4,1024]{2,1,0:T(4,128)(2,1)S(1)}, bf16[4,4,1024]{2,1,0:T(4,128)(2,1)}, u32[]{:S(2)}) copy-start(bf16[4,4,1024]{2,1,0:T(4,128)(2,1)} %param.19) | copy-start | bytes 98308
  39.1 8.7 %collective-permute-start.5 = (bf16[1056,128]{1,0:T(8,128)(2,1)S(1)}, bf16[1056,128]{1,0:T(8,128)(2,1)S(1)}, u32[]{:S(2)}, u32[]{:S(2)}) collective-permute-start(bf16[1056,128]{1,0:T(8,128)(2,1)S(1)} %shard_map.101), channel_id=1, source_target_pairs={{0,16},{1,17},{2,18},{3,19},{4,20},{5,21},{6,22},{7,23},{8,24},{9,... | collective-permute-start | bytes 811016 | tf_op jit(solution)/shard_map/ppermute | solution.py:39
  42.5 9.3 %collective-permute-start.7 = (bf16[1056,128]{1,0:T(8,128)(2,1)S(1)}, bf16[1056,128]{1,0:T(8,128)(2,1)S(1)}, u32[]{:S(2)}, u32[]{:S(2)}) collective-permute-start(bf16[1056,128]{1,0:T(8,128)(2,1)S(1)} %shard_map.102), channel_id=1, source_target_pairs={{0,144},{1,129},{2,146},{3,131},{4,148},{5,133},{6,150},{7,135},{8... | collective-permute-start | bytes 811016 | tf_op jit(solution)/shard_map/ppermute | solution.py:39

commit v2 on v1

v2 whole, which is shorter than its diff:
```python
import functools

import jax
import jax.numpy as jnp
from jax import lax
from jax.experimental import pallas as pl
from jax.experimental.pallas import tpu as pltpu
from jax.sharding import PartitionSpec as P

H = 64
KVH = 8
HD = 128
BLK = 128
GROUP = H // KVH
AXES = ("span", "rows")
MASKED = -1e30
SCALE = 1.4426950408889634 * HD ** (-0.5)
ROWS = 4
STEPS = 4
QR = GROUP * STEPS
NQ = ROWS * QR
TOTAL = KVH * NQ
EXT = 16
STAT = 32


def device_id(x, y, z, c):
    x, y, z, c = x % 4, y % 4, z % 8, c % 2
    return ((y % 2) * 4 + x) * 32 + (y // 2) * 16 + z * 2 + c


def send(value, target):
    pairs = [
        (device_id(x, y, z, c), device_id(*target(x, y, z, c)))
        for x in range(4)
        for y in range(4)
        for z in range(8)
        for c in range(2)
    ]
    return lax.ppermute(value, AXES, pairs)


def to_partner(x, y, z, c):
    return (x, y + 2, z, c)


def to_neighbour(x, y, z, c):
    return (x, y + 1 - 2 * c, z, c)


def from_neighbour(x, y, z, c):
    return (x, y - 1 + 2 * c, z, c)


def along_x(x, y, z, c):
    return (x + 1 - 2 * c, y, z, c)


def other_core(x, y, z, c):
    return (x, y, z, 1 - c)


def dot_nt(a, b):
    return lax.dot_general(a, b, (((1,), (1,)), ((), ())), preferred_element_type=jnp.float32)


def dot_nn(a, b):
    return lax.dot_general(a, b, (((1,), (0,)), ((), ())), preferred_element_type=jnp.float32)


def head_rows(ref, j):
    return jnp.concatenate([ref[r * 256 + j * QR : r * 256 + (j + 1) * QR, :] for r in range(ROWS)], axis=0)


def ext_column(q_ref, lane):
    ext = q_ref[TOTAL : TOTAL + ROWS * EXT, :].astype(jnp.float32)
    lanes = lax.broadcasted_iota(jnp.int32, ext.shape, 1)
    column = jnp.sum(jnp.where(lanes == lane, ext, 0.0), axis=1, keepdims=True)
    pieces = []
    for r in range(ROWS):
        piece = column[r * EXT : (r + 1) * EXT, :]
        pieces += [piece, piece]
    return jnp.concatenate(pieces, axis=0)


def pack_stats(stat):
    rows = stat.T[:KVH, :]
    hi = rows.astype(jnp.bfloat16)
    rest = rows - hi.astype(jnp.float32)
    mid = rest.astype(jnp.bfloat16)
    low = (rest - mid.astype(jnp.float32)).astype(jnp.bfloat16)
    pad = jnp.zeros_like(hi)
    return jnp.concatenate([hi, mid, low, pad], axis=0)


def unpack_stats(ref):
    rows = ref[TOTAL : TOTAL + STAT, :].astype(jnp.float32)
    rows = rows[:KVH] + rows[KVH : 2 * KVH] + rows[2 * KVH : 3 * KVH]
    full = jnp.concatenate([rows, jnp.zeros((NQ - KVH, NQ), jnp.float32)], axis=0)
    return full.T


def pipelined(stages, count):
    held = {}
    for time in range(count + len(stages) - 1):
        for s in range(len(stages)):
            i = time - s
            if 0 <= i < count:
                held[i] = stages[s](i, held.get(i))


def soften(parts):
    largest = jnp.max(functools.reduce(jnp.maximum, parts), axis=1, keepdims=True)
    weights = [jnp.exp2((part - largest) * SCALE) for part in parts]
    mass = jnp.sum(functools.reduce(jnp.add, weights), axis=1, keepdims=True)
    rounded = jnp.concatenate([w.astype(jnp.bfloat16) for w in weights], axis=1)
    return rounded, largest, mass


def store_head(out_ref, j, result):
    for r in range(ROWS):
        out_ref[r * 256 + j * QR : r * 256 + (j + 1) * QR, :] = result[r * QR : (r + 1) * QR, :].astype(out_ref.dtype)


def head(j):
    return slice(j * HD, (j + 1) * HD)


def pack_kernel(
    q_hbm, k_hbm, v_hbm, mask_hbm, branch_hbm, packed_ref, first_ref, second_ref, mask_ref, branch_ref, sems
):
    core = lax.rem(lax.axis_index("rows"), 2)
    small = [
        pltpu.make_async_copy(mask_hbm, mask_ref, sems.at[1]),
        pltpu.make_async_copy(branch_hbm, branch_ref, sems.at[2]),
    ]
    queries = pltpu.make_async_copy(q_hbm, packed_ref.at[pl.ds(0, TOTAL)], sems.at[0])

    def halves(one, two):
        return (pltpu.make_async_copy(one, first_ref, sems.at[3]), pltpu.make_async_copy(two, second_ref, sems.at[4]))

    for copy in small:
        copy.start()
    queries.start()

    @pl.when(core == 0)
    def _():
        for copy in halves(k_hbm, v_hbm):
            copy.start()

    @pl.when(core == 1)
    def _():
        for copy in halves(v_hbm, k_hbm):
            copy.start()

    shape = (ROWS, HD)
    lanes = lax.broadcasted_iota(jnp.int32, shape, 1)
    rows = lax.broadcasted_iota(jnp.int32, shape, 0)
    extra = jnp.zeros(shape, jnp.int32)
    for copy in small:
        copy.wait()
    for i in range(KVH):
        extra = jnp.where(lanes == i, mask_ref[:, i : i + 1], extra)
    for r in range(ROWS):
        extra = jnp.where((lanes == KVH) & (rows == r), branch_ref[:, r : r + 1], extra)
    extra = extra.astype(jnp.float32)
    for r in range(ROWS):
        tile = jnp.broadcast_to(extra[r : r + 1, :], (EXT, HD)).astype(jnp.bfloat16)
        packed_ref[TOTAL + r * EXT : TOTAL + (r + 1) * EXT, :] = tile
    queries.wait()
    for copy in halves(k_hbm, v_hbm):
        copy.wait()


def load_kernel(*refs):
    count = len(refs) // 2
    sems = refs[-1]
    copies = [pltpu.make_async_copy(refs[i], refs[count + i], sems.at[i]) for i in range(count)]
    for copy in copies:
        copy.start()
    for copy in copies:
        copy.wait()


def suffix_kernel(len_ref, q_ref, k_ref, v_ref, out_ref):
    slots = k_ref.shape[1]
    second = ext_column(q_ref, KVH) > 0.5
    wide = jnp.broadcast_to(second, (NQ, HD))
    length = jnp.where(second, len_ref[:, 1:2], len_ref[:, 0:1])
    allowed = lax.broadcasted_iota(jnp.int32, (NQ, slots), 1) < length
    lanes = lax.broadcasted_iota(jnp.int32, (NQ, 128), 1)
    zero = jnp.zeros((NQ, HD), jnp.bfloat16)
    stats = [jnp.zeros((NQ, 128), jnp.float32)]

    def score(j, _):
        query = head_rows(q_ref, j)
        query = jnp.concatenate([jnp.where(wide, zero, query), jnp.where(wide, query, zero)], axis=1)
        return dot_nt(query, jnp.concatenate([k_ref[0, :, head(j)], k_ref[1, :, head(j)]], axis=1))

    def weigh(j, scores):
        return soften([jnp.where(allowed, scores, MASKED)])

    def mix(j, held):
        rounded, largest, mass = held
        mixed = dot_nn(rounded, jnp.concatenate([v_ref[0, :, head(j)], v_ref[1, :, head(j)]], axis=1))
        mixed = jnp.where(second, mixed[:, HD:], mixed[:, :HD])
        store_head(out_ref, j, mixed * (1.0 / mass))
        stats[0] = jnp.where(lanes == j, largest * SCALE + jnp.log2(mass), stats[0])

    pipelined((score, weigh, mix), KVH)
    out_ref[TOTAL : TOTAL + STAT, :] = pack_stats(stats[0])


def prefix_kernel(with_new, *refs):
    q_ref, k_own, v_own, near_one, near_two, far_one, far_two, half_own, half_other = refs[:9]
    if with_new:
        nk_ref, nv_ref, out_ref, stat_ref = refs[9:]
    else:
        (out_ref,) = refs[9:]
    span = lax.axis_index("span")
    core = lax.rem(lax.axis_index("rows"), 2)
    x = lax.rem(span, 4)
    first = span - x
    allowed = [ext_column(q_ref, first + lax.rem(x + offset, 4)) > 0.5 for offset in (0, 3, 1, 2)]
    lanes = lax.broadcasted_iota(jnp.int32, (NQ, 128), 1)
    on_second = jnp.full((BLK, HD), core) == 1
    stats = [jnp.zeros((NQ, 128), jnp.float32)]
    if with_new:
        row_of = lax.broadcasted_iota(jnp.int32, (NQ, 128), 0)
        same_row = (row_of // QR) == (lanes // (KVH * STEPS))
        new_base = same_row & ((lanes % STEPS) <= (row_of % STEPS))
        new_head = (lanes // STEPS) % KVH

    def by_core(j, zero, one):
        return jnp.where(on_second, one[:, head(j)], zero[:, head(j)])

    def score(j, _):
        keys = [
            k_own[:, head(j)],
            by_core(j, near_one, far_one),
            by_core(j, far_two, near_two),
            by_core(j, half_own, half_other),
        ]
        if with_new:
            keys.append(nk_ref[...])
        return dot_nt(head_rows(q_ref, j), jnp.concatenate(keys, axis=0))

    def weigh(j, scores):
        parts = [jnp.where(allowed[i], scores[:, i * BLK : (i + 1) * BLK], MASKED) for i in range(4)]
        if with_new:
            parts.append(jnp.where(new_base & (new_head == j), scores[:, 4 * BLK :], MASKED))
        return soften(parts)

    def mix(j, held):
        rounded, largest, mass = held
        values = [
            v_own[:, head(j)],
            by_core(j, near_two, far_two),
            by_core(j, far_one, near_one),
            by_core(j, half_other, half_own),
        ]
        if with_new:
            values.append(nv_ref[...])
        mixed = dot_nn(rounded, jnp.concatenate(values, axis=0))
        store_head(out_ref, j, mixed * (1.0 / mass))
        stats[0] = jnp.where(lanes == j, largest * SCALE + jnp.log2(mass), stats[0])

    pipelined((score, weigh, mix), KVH)
    if with_new:
        stat_ref[...] = stats[0]
    else:
        out_ref[TOTAL : TOTAL + STAT, :] = pack_stats(stats[0])


def combine_kernel(own_ref, stat_ref, far_ref, near_ref, out_ref):
    own, far, near = stat_ref[...], unpack_stats(far_ref), unpack_stats(near_ref)
    top = jnp.maximum(jnp.maximum(own, far), near)
    own, far, near = jnp.exp2(own - top), jnp.exp2(far - top), jnp.exp2(near - top)
    scale = 1.0 / (own + far + near)
    own, far, near = own * scale, far * scale, near * scale
    for j in range(KVH):
        for r in range(ROWS):
            rows = slice(r * 256 + j * QR, r * 256 + (j + 1) * QR)
            part = slice(r * QR, (r + 1) * QR)
            out_ref[rows, :] = (
                own_ref[rows, :] * own[part, j : j + 1]
                + far_ref[rows, :].astype(jnp.float32) * far[part, j : j + 1]
                + near_ref[rows, :].astype(jnp.float32) * near[part, j : j + 1]
            ).astype(jnp.bfloat16)


VMEM = pl.BlockSpec(memory_space=pltpu.VMEM)
HBM = pl.BlockSpec(memory_space=pltpu.HBM)


def vmem(shape, dtype=jnp.bfloat16):
    return pltpu.VMEM(shape, dtype)


PACKED = vmem((TOTAL + STAT, HD))


def in_hbm(*values):
    return tuple(pltpu.with_memory_space_constraint(value, pltpu.HBM) for value in values)


def call(kernel, args, specs, out, scratch=()):
    return pl.pallas_call(
        kernel,
        out_shape=out,
        in_specs=specs,
        out_specs=jax.tree.map(lambda _: VMEM, out),
        scratch_shapes=list(scratch),
        cost_estimate=pl.CostEstimate(flops=1, bytes_accessed=1, transcendentals=0),
        compiler_params=pltpu.CompilerParams(vmem_limit_bytes=16 << 20),
    )(*args)


def heads_first(value, heads):
    rows, steps, _ = value.shape
    return value.reshape(rows, steps, heads, HD).transpose(0, 2, 1, 3).reshape(rows * heads * steps, HD)


def on_device(
    queries,
    prefix_keys,
    prefix_values,
    prefix_mask,
    suffix_keys,
    suffix_values,
    suffix_len,
    row_branch,
    new_keys,
    new_values,
):
    block = prefix_keys.shape
    packed, one, two = call(
        pack_kernel,
        in_hbm(heads_first(queries, H), prefix_keys, prefix_values, prefix_mask, row_branch.reshape(1, ROWS)),
        [HBM] * 5,
        (vmem((TOTAL + ROWS * EXT, HD)), vmem(block), vmem(block)),
        [
            pltpu.VMEM(prefix_mask.shape, jnp.int32),
            pltpu.VMEM((1, ROWS), jnp.int32),
            pltpu.SemaphoreType.DMA((5,)),
        ],
    )
    near_one = send(one, along_x)
    far_queries = send(packed, to_partner)
    near_two = send(two, along_x)
    half_own = send(near_one, along_x)
    far_one = send(near_one, other_core)
    far_two = send(near_two, other_core)

    stored = (suffix_len.reshape(1, 2), suffix_keys, suffix_values)
    stored, packed = lax.optimization_barrier((stored, packed))
    stored = call(
        load_kernel,
        in_hbm(*stored),
        [HBM] * 3,
        tuple(vmem(value.shape, value.dtype) for value in stored),
        [pltpu.SemaphoreType.DMA((3,))],
    )
    later, _ = lax.optimization_barrier((packed, near_one))
    near_queries = send(later, to_neighbour)
    suffix = call(suffix_kernel, (stored[0], far_queries, stored[1], stored[2]), [VMEM] * 4, PACKED)
    half_own, _ = lax.optimization_barrier((half_own, suffix))
    half_other = send(half_own, other_core)
    suffix = send(suffix, to_partner)

    blocks = (prefix_keys, prefix_values, near_one, near_two, far_one, far_two, half_own, half_other)
    near = call(functools.partial(prefix_kernel, False), (near_queries,) + blocks, [VMEM] * 9, PACKED)
    near = send(near, from_neighbour)
    own, stat = call(
        functools.partial(prefix_kernel, True),
        (packed,) + blocks + (heads_first(new_keys, KVH), heads_first(new_values, KVH)),
        [VMEM] * 11,
        (vmem((TOTAL, HD), jnp.float32), vmem((NQ, 128), jnp.float32)),
    )
    merged = call(
        combine_kernel, (own, stat, suffix, near), [VMEM] * 4, jax.ShapeDtypeStruct((TOTAL, HD), jnp.bfloat16)
    )
    merged = merged.reshape(ROWS, H, STEPS, HD).transpose(0, 2, 1, 3)
    return merged.reshape(queries.shape)


def solution(mesh):
    return jax.shard_map(
        on_device,
        mesh=mesh,
        in_specs=(
            P(AXES, None, None),
            P("span", None),
            P("span", None),
            P(AXES, None),
            P(AXES, None, None),
            P(AXES, None, None),
            P(AXES),
            P(AXES),
            P(AXES, None, None),
            P(AXES, None, None),
        ),
        out_specs=P(AXES, None, None),
        check_vma=False,
    )
```

time: 53.4 us -> 33.8 us (0.63)
  waiting for transfers between devices: 23.1 us -> 7.43 us
  starting transfers between devices: 8.75 us -> 16 us
  other arithmetic: 5.36 us -> 0 us
  Pallas kernels: 14 us -> 10.1 us
  local copies, waits for them, and re-layouts: 1.74 us -> 0.01 us
    ppermute x8 -> x10, waiting for transfers between devices: 23.1 us -> 7.43 us  [send(): return lax.ppermute(value, AXES, pairs)]
    ppermute x8 -> x10, starting transfers between devices: 8.75 us -> 16 us  [send(): return lax.ppermute(value, AXES, pairs)]
    pallas_call x4 -> x6, Pallas kernels: 14 us -> 10.1 us  [call(): pl.pallas_call(kernel, out_shape=out, in_specs=specs, out_specs=jax.tree....]
    another operation x2 -> x0, other arithmetic: 1.91 us -> none  [the longest x1 1.23 us: on_device(): both = jnp.stack([prefix_keys, prefix_values])]
    squeeze x1 -> x0, other arithmetic: 1.75 us -> none  [on_device(): lax.dynamic_index_in_dim(both, core, 0, keepdims=False)]
    unnamed x14 -> x8, local copies, waits for them, and re-layouts: 1.62 us -> 0.01 us
    concatenate x2 -> x0, other arithmetic: 1.05 us -> none  [the longest x1 0.97 us: on_device(): packed = jnp.concatenate([heads_first(queries, H), extra], axis=0)]
    broadcast_in_dim x1 -> x0, other arithmetic: 0.66 us -> none  [on_device(): row_branch[:, None]]
  transfers between devices with their start and end apart: 8 -> 10, of which waited for: 4 -> 2; matrix products, arithmetic and copies ran while one was open for 8% -> 0% of each run, Pallas kernels for 24% -> 22%
where the time goes in v2:
time: 33.8 us; the launch traced here: 33.7 us
  starting transfers between devices  16 us (47%)
  Pallas kernels  10.1 us (30%)
  waiting for transfers between devices  7.43 us (22%)
    ppermute x10, starting transfers between devices, send(): return lax.ppermute(value, AXES, pairs)  16 us
    pallas_call x6, Pallas kernels, call(): pl.pallas_call(kernel, out_shape=out, in_specs=specs, out_specs=jax.tree....  10.1 us
    ppermute x10, waiting for transfers between devices, send(): return lax.ppermute(value, AXES, pairs)  7.43 us
  transfers between devices with their start and end apart: 10, of which 2 were waited for; matrix products, arithmetic and copies ran while one was open for 0% of the time, Pallas kernels for 22%

profile of v2, /device:TPU:1, one launch (start us, length us, event | category | flops | bytes accessed | tf_op | source)
XLA Modules:
  0.0 33.7 jit_solution(17899321296873918765)
XLA Ops:
  0.0 1.2 %shard_map.100 = (bf16[1088,128]{1,0:T(8,128)(2,1)S(1)}, bf16[128,1024]{1,0:T(8,128)(2,1)S(1)}, bf16[128,1024]{1,0:T(8,128)(2,1)S(1)}) custom-call(bf16[1024,128]{1,0:T(8,128)(2,1)} %bitcast.24, bf16[128,1024]{1,0:T(8,128)(2,1)} %refs_1_.4, bf16[128,1024]{1,0:T(8,128)(2,1)} %refs_2_.4, s32[4,8]{1,0:T(4,128)} %mask_hbm.1, s32[1,4]{1,0:T(1,128)} %bitcast.26), custom_call_target="tpu_custom_call" | custom-call | flops 1 | bytes 1 | tf_op jit(solution)/shard_map/pallas_call | solution.py:308
  1.2 3.4 %collective-permute-start = (bf16[128,1024]{1,0:T(8,128)(2,1)S(1)}, bf16[128,1024]{1,0:T(8,128)(2,1)S(1)}, u32[]{:S(2)}, u32[]{:S(2)}) collective-permute-start(bf16[128,1024]{1,0:T(8,128)(2,1)S(1)} %get-tuple-element.21), channel_id=1, source_target_pairs={{0,32},{1,97},{2,34},{3,99},{4,36},{5,101},{6,38},{7,103},{8,40},{... | collective-permute-start | bytes 786440 | tf_op jit(solution)/shard_map/ppermute | solution.py:40
  4.6 2.9 %collective-permute-start.5 = (bf16[1088,128]{1,0:T(8,128)(2,1)S(1)}, bf16[1088,128]{1,0:T(8,128)(2,1)S(1)}, u32[]{:S(2)}, u32[]{:S(2)}) collective-permute-start(bf16[1088,128]{1,0:T(8,128)(2,1)S(1)} %get-tuple-element.32.refs_0_), channel_id=1, source_target_pairs={{0,16},{1,17},{2,18},{3,19},{4,20},{5,21},{6,22},{7,23},{8,24},{9,... | collective-permute-start | bytes 835592 | tf_op jit(solution)/shard_map/ppermute | solution.py:40
  7.5 0.5 %collective-permute-start.1 = (bf16[128,1024]{1,0:T(8,128)(2,1)S(1)}, bf16[128,1024]{1,0:T(8,128)(2,1)S(1)}, u32[]{:S(2)}, u32[]{:S(2)}) collective-permute-start(bf16[128,1024]{1,0:T(8,128)(2,1)S(1)} %get-tuple-element.22), channel_id=1, source_target_pairs={{0,32},{1,97},{2,34},{3,99},{4,36},{5,101},{6,38},{7,103},{8,40},{... | collective-permute-start | bytes 786440 | tf_op jit(solution)/shard_map/ppermute | solution.py:40
  8.0 0.0 collective-permute-done.refs_3_
  8.0 3.0 %collective-permute-start.4 = (bf16[128,1024]{1,0:T(8,128)(2,1)S(1)}, bf16[128,1024]{1,0:T(8,128)(2,1)S(1)}, u32[]{:S(2)}, u32[]{:S(2)}) collective-permute-start(bf16[128,1024]{1,0:T(8,128)(2,1)S(1)} %collective-permute-done.refs_3_), channel_id=1, source_target_pairs={{0,32},{1,97},{2,34},{3,99},{4,36},{5,101},{6,38},{7,103},{8,40},{... | collective-permute-start | bytes 786440 | tf_op jit(solution)/shard_map/ppermute | solution.py:40
  11.0 3.0 %collective-permute-start.8 = (bf16[1088,128]{1,0:T(8,128)(2,1)S(1)}, bf16[1088,128]{1,0:T(8,128)(2,1)S(1)}, u32[]{:S(2)}, u32[]{:S(2)}) collective-permute-start(bf16[1088,128]{1,0:T(8,128)(2,1)S(1)} %get-tuple-element.32.refs_0_), channel_id=1, source_target_pairs={{0,128},{1,145},{2,130},{3,147},{4,132},{5,149},{6,134},{7,151},{8... | collective-permute-start | bytes 835592 | tf_op jit(solution)/shard_map/ppermute | solution.py:40
  14.0 2.3 %shard_map.101 = (s32[1,2]{1,0:T(1,128)S(1)}, bf16[2,512,1024]{2,1,0:T(8,128)(2,1)S(1)}, bf16[2,512,1024]{2,1,0:T(8,128)(2,1)S(1)}) custom-call(s32[1,2]{1,0:T(1,128)} %bitcast.25, bf16[2,512,1024]{2,1,0:T(8,128)(2,1)} %refs_1_.2, bf16[2,512,1024]{2,1,0:T(8,128)(2,1)} %refs_2_.2), custom_call_target="tpu_custom_call" | custom-call | flops 1 | bytes 1 | tf_op jit(solution)/shard_map/pallas_call | solution.py:308
  16.3 0.1 collective-permute-start.2
  16.4 0.0 collective-permute-done.1.refs_4_
  16.4 0.5 %collective-permute-start.3 = (bf16[128,1024]{1,0:T(8,128)(2,1)S(1)}, bf16[128,1024]{1,0:T(8,128)(2,1)S(1)}, u32[]{:S(2)}, u32[]{:S(2)}) collective-permute-start(bf16[128,1024]{1,0:T(8,128)(2,1)S(1)} %collective-permute-done.1.refs_4_), channel_id=1, source_target_pairs={{0,1},{1,0},{2,3},{3,2},{4,5},{5,4},{6,7},{7,6},{8,9},{9,8},{10,11... | collective-permute-start | bytes 786440 | tf_op jit(solution)/shard_map/ppermute | solution.py:40
  16.9 0.0 collective-permute-done.5.q_ref
  16.9 0.0 copy-start
  16.9 0.0 copy-start.1
  16.9 1.7 %shard_map.102 = bf16[1056,128]{1,0:T(8,128)(2,1)S(1)} custom-call(s32[1,2]{1,0:T(1,128)S(1)} %get-tuple-element.26.len_ref, bf16[1088,128]{1,0:T(8,128)(2,1)S(1)} %collective-permute-done.5.q_ref, bf16[2,512,1024]{2,1,0:T(8,128)(2,1)S(1)} %get-tuple-element.27.k_ref, bf16[2,512,1024]{2,1,0:T(8,128)(2,1)S(1)} %get-tuple-element.28.v_ref), custom_call_target="tpu_custom_call" | custom-call | flops 1 | bytes 1 | tf_op jit(solution)/shard_map/pallas_call | solution.py:308
  18.7 0.0 collective-permute-done.4.refs_7_
  18.7 1.0 %collective-permute-start.6 = (bf16[128,1024]{1,0:T(8,128)(2,1)S(1)}, bf16[128,1024]{1,0:T(8,128)(2,1)S(1)}, u32[]{:S(2)}, u32[]{:S(2)}) collective-permute-start(bf16[128,1024]{1,0:T(8,128)(2,1)S(1)} %collective-permute-done.4.refs_7_), channel_id=1, source_target_pairs={{0,1},{1,0},{2,3},{3,2},{4,5},{5,4},{6,7},{7,6},{8,9},{9,8},{10,11... | collective-permute-start | bytes 786440 | tf_op jit(solution)/shard_map/ppermute | solution.py:40
  19.7 1.2 %collective-permute-start.7 = (bf16[1056,128]{1,0:T(8,128)(2,1)S(1)}, bf16[1056,128]{1,0:T(8,128)(2,1)S(1)}, u32[]{:S(2)}, u32[]{:S(2)}) collective-permute-start(bf16[1056,128]{1,0:T(8,128)(2,1)S(1)} %shard_map.102), channel_id=1, source_target_pairs={{0,16},{1,17},{2,18},{3,19},{4,20},{5,21},{6,22},{7,23},{8,24},{9,... | collective-permute-start | bytes 811016 | tf_op jit(solution)/shard_map/ppermute | solution.py:40
  20.9 0.0 collective-permute-done.2.refs_5_
  20.9 0.0 collective-permute-done.3.refs_6_
  20.9 0.0 collective-permute-done.8.refs_0_
  20.9 0.0 collective-permute-done.6.refs_8_
  20.9 0.0 copy-done
  20.9 0.0 copy-done.1
  20.9 1.6 %shard_map.104 = bf16[1056,128]{1,0:T(8,128)(2,1)S(1)} custom-call(bf16[1088,128]{1,0:T(8,128)(2,1)S(1)} %collective-permute-done.8.refs_0_, bf16[128,1024]{1,0:T(8,128)(2,1)S(1)} %copy-done, bf16[128,1024]{1,0:T(8,128)(2,1)S(1)} %copy-done.1, bf16[128,1024]{1,0:T(8,128)(2,1)S(1)} %collective-permute-done.refs_3_, ...), custom_call_target="tpu_custom_call" | custom-call | flops 1 | bytes 1 | tf_op jit(solution)/shard_map/pallas_call | solution.py:308
  22.5 0.4 %collective-permute-start.9 = (bf16[1056,128]{1,0:T(8,128)(2,1)S(1)}, bf16[1056,128]{1,0:T(8,128)(2,1)S(1)}, u32[]{:S(2)}, u32[]{:S(2)}) collective-permute-start(bf16[1056,128]{1,0:T(8,128)(2,1)S(1)} %shard_map.104), channel_id=1, source_target_pairs={{0,144},{1,129},{2,146},{3,131},{4,148},{5,133},{6,150},{7,135},{8... | collective-permute-start | bytes 811016 | tf_op jit(solution)/shard_map/ppermute | solution.py:40
  23.0 0.0 copy-done.2
  23.0 0.0 copy-done.3
  23.0 1.9 %shard_map.103 = (f32[1024,128]{1,0:T(8,128)S(1)}, f32[128,128]{1,0:T(8,128)S(1)}) custom-call(bf16[1088,128]{1,0:T(8,128)(2,1)S(1)} %get-tuple-element.32.refs_0_, bf16[128,1024]{1,0:T(8,128)(2,1)S(1)} %copy-done, bf16[128,1024]{1,0:T(8,128)(2,1)S(1)} %copy-done.1, bf16[128,1024]{1,0:T(8,128)(2,1)S(1)} %collective-permute-done.refs_3_, ...), custom_call_target="tpu_custom_call" | custom-call | flops 1 | bytes 1 | tf_op jit(solution)/shard_map/pallas_call | solution.py:308
  24.9 4.5 %collective-permute-done.7.far_ref = bf16[1056,128]{1,0:T(8,128)(2,1)S(1)} collective-permute-done((bf16[1056,128]{1,0:T(8,128)(2,1)S(1)}, bf16[1056,128]{1,0:T(8,128)(2,1)S(1)}, u32[]{:S(2)}, u32[]{:S(2)}) %collective-permute-start.7) | collective-permute-done | bytes 270368 | tf_op jit(solution)/shard_map/ppermute | solution.py:40
  29.3 2.9 %collective-permute-done.9.near_ref = bf16[1056,128]{1,0:T(8,128)(2,1)S(1)} collective-permute-done((bf16[1056,128]{1,0:T(8,128)(2,1)S(1)}, bf16[1056,128]{1,0:T(8,128)(2,1)S(1)}, u32[]{:S(2)}, u32[]{:S(2)}) %collective-permute-start.9) | collective-permute-done | bytes 270368 | tf_op jit(solution)/shard_map/ppermute | solution.py:40
  32.3 1.4 %shard_map.105 = bf16[1024,128]{1,0:T(8,128)(2,1)} custom-call(f32[1024,128]{1,0:T(8,128)S(1)} %get-tuple-element.30.own_ref, f32[128,128]{1,0:T(8,128)S(1)} %get-tuple-element.31.stat_ref, bf16[1056,128]{1,0:T(8,128)(2,1)S(1)} %collective-permute-done.7.far_ref, bf16[1056,128]{1,0:T(8,128)(2,1)S(1)} %collective-permute-done.9.near_ref), custom_call_target="tpu_custom_call" | custom-call | flops 1 | bytes 1 | tf_op jit(solution)/shard_map/pallas_call | solution.py:308
  (2 shorter events, 0.0 us)
Async XLA Ops:
  1.2 6.9 %collective-permute-start = (bf16[128,1024]{1,0:T(8,128)(2,1)S(1)}, bf16[128,1024]{1,0:T(8,128)(2,1)S(1)}, u32[]{:S(2)}, u32[]{:S(2)}) collective-permute-start(bf16[128,1024]{1,0:T(8,128)(2,1)S(1)} %get-tuple-element.21), channel_id=1, source_target_pairs={{0,32},{1,97},{2,34},{3,99},{4,36},{5,101},{6,38},{7,103},{8,40},{... | collective-permute-start | bytes 786440 | tf_op jit(solution)/shard_map/ppermute | solution.py:40
  4.6 12.3 %collective-permute-start.5 = (bf16[1088,128]{1,0:T(8,128)(2,1)S(1)}, bf16[1088,128]{1,0:T(8,128)(2,1)S(1)}, u32[]{:S(2)}, u32[]{:S(2)}) collective-permute-start(bf16[1088,128]{1,0:T(8,128)(2,1)S(1)} %get-tuple-element.32.refs_0_), channel_id=1, source_target_pairs={{0,16},{1,17},{2,18},{3,19},{4,20},{5,21},{6,22},{7,23},{8,24},{9,... | collective-permute-start | bytes 835592 | tf_op jit(solution)/shard_map/ppermute | solution.py:40
  7.5 8.9 %collective-permute-start.1 = (bf16[128,1024]{1,0:T(8,128)(2,1)S(1)}, bf16[128,1024]{1,0:T(8,128)(2,1)S(1)}, u32[]{:S(2)}, u32[]{:S(2)}) collective-permute-start(bf16[128,1024]{1,0:T(8,128)(2,1)S(1)} %get-tuple-element.22), channel_id=1, source_target_pairs={{0,32},{1,97},{2,34},{3,99},{4,36},{5,101},{6,38},{7,103},{8,40},{... | collective-permute-start | bytes 786440 | tf_op jit(solution)/shard_map/ppermute | solution.py:40
  8.0 10.6 %collective-permute-start.4 = (bf16[128,1024]{1,0:T(8,128)(2,1)S(1)}, bf16[128,1024]{1,0:T(8,128)(2,1)S(1)}, u32[]{:S(2)}, u32[]{:S(2)}) collective-permute-start(bf16[128,1024]{1,0:T(8,128)(2,1)S(1)} %collective-permute-done.refs_3_), channel_id=1, source_target_pairs={{0,32},{1,97},{2,34},{3,99},{4,36},{5,101},{6,38},{7,103},{8,40},{... | collective-permute-start | bytes 786440 | tf_op jit(solution)/shard_map/ppermute | solution.py:40
  11.0 9.9 %collective-permute-start.8 = (bf16[1088,128]{1,0:T(8,128)(2,1)S(1)}, bf16[1088,128]{1,0:T(8,128)(2,1)S(1)}, u32[]{:S(2)}, u32[]{:S(2)}) collective-permute-start(bf16[1088,128]{1,0:T(8,128)(2,1)S(1)} %get-tuple-element.32.refs_0_), channel_id=1, source_target_pairs={{0,128},{1,145},{2,130},{3,147},{4,132},{5,149},{6,134},{7,151},{8... | collective-permute-start | bytes 835592 | tf_op jit(solution)/shard_map/ppermute | solution.py:40
  16.3 4.5 %collective-permute-start.2 = (bf16[128,1024]{1,0:T(8,128)(2,1)S(1)}, bf16[128,1024]{1,0:T(8,128)(2,1)S(1)}, u32[]{:S(2)}, u32[]{:S(2)}) collective-permute-start(bf16[128,1024]{1,0:T(8,128)(2,1)S(1)} %collective-permute-done.refs_3_), channel_id=1, source_target_pairs={{0,1},{1,0},{2,3},{3,2},{4,5},{5,4},{6,7},{7,6},{8,9},{9,8},{10,11... | collective-permute-start | bytes 786440 | tf_op jit(solution)/shard_map/ppermute | solution.py:40
  16.4 4.4 %collective-permute-start.3 = (bf16[128,1024]{1,0:T(8,128)(2,1)S(1)}, bf16[128,1024]{1,0:T(8,128)(2,1)S(1)}, u32[]{:S(2)}, u32[]{:S(2)}) collective-permute-start(bf16[128,1024]{1,0:T(8,128)(2,1)S(1)} %collective-permute-done.1.refs_4_), channel_id=1, source_target_pairs={{0,1},{1,0},{2,3},{3,2},{4,5},{5,4},{6,7},{7,6},{8,9},{9,8},{10,11... | collective-permute-start | bytes 786440 | tf_op jit(solution)/shard_map/ppermute | solution.py:40
  16.9 4.0 %copy-start = (bf16[128,1024]{1,0:T(8,128)(2,1)S(1)}, bf16[128,1024]{1,0:T(8,128)(2,1)}, u32[]{:S(2)}) copy-start(bf16[128,1024]{1,0:T(8,128)(2,1)} %refs_1_.4) | copy-start | bytes 786436
  16.9 4.0 %copy-start.1 = (bf16[128,1024]{1,0:T(8,128)(2,1)S(1)}, bf16[128,1024]{1,0:T(8,128)(2,1)}, u32[]{:S(2)}) copy-start(bf16[128,1024]{1,0:T(8,128)(2,1)} %refs_2_.4) | copy-start | bytes 786436
  18.7 4.3 %copy-start.2 = (bf16[4,4,1024]{2,1,0:T(4,128)(2,1)S(1)}, bf16[4,4,1024]{2,1,0:T(4,128)(2,1)}, u32[]{:S(2)}) copy-start(bf16[4,4,1024]{2,1,0:T(4,128)(2,1)} %param.18) | copy-start | bytes 98308
  18.7 4.3 %copy-start.3 = (bf16[4,4,1024]{2,1,0:T(4,128)(2,1)S(1)}, bf16[4,4,1024]{2,1,0:T(4,128)(2,1)}, u32[]{:S(2)}) copy-start(bf16[4,4,1024]{2,1,0:T(4,128)(2,1)} %param.19) | copy-start | bytes 98308
  18.7 2.2 %collective-permute-start.6 = (bf16[128,1024]{1,0:T(8,128)(2,1)S(1)}, bf16[128,1024]{1,0:T(8,128)(2,1)S(1)}, u32[]{:S(2)}, u32[]{:S(2)}) collective-permute-start(bf16[128,1024]{1,0:T(8,128)(2,1)S(1)} %collective-permute-done.4.refs_7_), channel_id=1, source_target_pairs={{0,1},{1,0},{2,3},{3,2},{4,5},{5,4},{6,7},{7,6},{8,9},{9,8},{10,11... | collective-permute-start | bytes 786440 | tf_op jit(solution)/shard_map/ppermute | solution.py:40
  19.7 9.7 %collective-permute-start.7 = (bf16[1056,128]{1,0:T(8,128)(2,1)S(1)}, bf16[1056,128]{1,0:T(8,128)(2,1)S(1)}, u32[]{:S(2)}, u32[]{:S(2)}) collective-permute-start(bf16[1056,128]{1,0:T(8,128)(2,1)S(1)} %shard_map.102), channel_id=1, source_target_pairs={{0,16},{1,17},{2,18},{3,19},{4,20},{5,21},{6,22},{7,23},{8,24},{9,... | collective-permute-start | bytes 811016 | tf_op jit(solution)/shard_map/ppermute | solution.py:40
  22.5 9.7 %collective-permute-start.9 = (bf16[1056,128]{1,0:T(8,128)(2,1)S(1)}, bf16[1056,128]{1,0:T(8,128)(2,1)S(1)}, u32[]{:S(2)}, u32[]{:S(2)}) collective-permute-start(bf16[1056,128]{1,0:T(8,128)(2,1)S(1)} %shard_map.104), channel_id=1, source_target_pairs={{0,144},{1,129},{2,146},{3,131},{4,148},{5,133},{6,150},{7,135},{8... | collective-permute-start | bytes 811016 | tf_op jit(solution)/shard_map/ppermute | solution.py:40

commit v3 on v2

--- a/solution.py
+++ b/solution.py
@@ -126,33 +126,14 @@
     return slice(j * HD, (j + 1) * HD)
 
 
-def pack_kernel(
-    q_hbm, k_hbm, v_hbm, mask_hbm, branch_hbm, packed_ref, first_ref, second_ref, mask_ref, branch_ref, sems
-):
-    core = lax.rem(lax.axis_index("rows"), 2)
+def pack_kernel(q_hbm, mask_hbm, branch_hbm, packed_ref, mask_ref, branch_ref, sems):
+    queries = pltpu.make_async_copy(q_hbm, packed_ref.at[pl.ds(0, TOTAL)], sems.at[0])
     small = [
         pltpu.make_async_copy(mask_hbm, mask_ref, sems.at[1]),
         pltpu.make_async_copy(branch_hbm, branch_ref, sems.at[2]),
     ]
-    queries = pltpu.make_async_copy(q_hbm, packed_ref.at[pl.ds(0, TOTAL)], sems.at[0])
-
-    def halves(one, two):
-        return (pltpu.make_async_copy(one, first_ref, sems.at[3]), pltpu.make_async_copy(two, second_ref, sems.at[4]))
-
-    for copy in small:
+    for copy in small + [queries]:
         copy.start()
-    queries.start()
-
-    @pl.when(core == 0)
-    def _():
-        for copy in halves(k_hbm, v_hbm):
-            copy.start()
-
-    @pl.when(core == 1)
-    def _():
-        for copy in halves(v_hbm, k_hbm):
-            copy.start()
-
     shape = (ROWS, HD)
     lanes = lax.broadcasted_iota(jnp.int32, shape, 1)
     rows = lax.broadcasted_iota(jnp.int32, shape, 0)
@@ -168,8 +149,6 @@
         tile = jnp.broadcast_to(extra[r : r + 1, :], (EXT, HD)).astype(jnp.bfloat16)
         packed_ref[TOTAL + r * EXT : TOTAL + (r + 1) * EXT, :] = tile
     queries.wait()
-    for copy in halves(k_hbm, v_hbm):
-        copy.wait()
 
 
 def load_kernel(*refs):
@@ -212,7 +191,7 @@
 
 
 def prefix_kernel(with_new, *refs):
-    q_ref, k_own, v_own, near_one, near_two, far_one, far_two, half_own, half_other = refs[:9]
+    q_ref, k_own, v_own, k_near, v_near, k_far, v_far, k_next, v_next = refs[:9]
     if with_new:
         nk_ref, nv_ref, out_ref, stat_ref = refs[9:]
     else:
@@ -221,9 +200,9 @@
     core = lax.rem(lax.axis_index("rows"), 2)
     x = lax.rem(span, 4)
     first = span - x
-    allowed = [ext_column(q_ref, first + lax.rem(x + offset, 4)) > 0.5 for offset in (0, 3, 1, 2)]
+    offsets = (0, 3 + 2 * core, 5 - 2 * core, 2)
+    allowed = [ext_column(q_ref, first + lax.rem(x + offset, 4)) > 0.5 for offset in offsets]
     lanes = lax.broadcasted_iota(jnp.int32, (NQ, 128), 1)
-    on_second = jnp.full((BLK, HD), core) == 1
     stats = [jnp.zeros((NQ, 128), jnp.float32)]
     if with_new:
         row_of = lax.broadcasted_iota(jnp.int32, (NQ, 128), 0)
@@ -231,16 +210,8 @@
         new_base = same_row & ((lanes % STEPS) <= (row_of % STEPS))
         new_head = (lanes // STEPS) % KVH
 
-    def by_core(j, zero, one):
-        return jnp.where(on_second, one[:, head(j)], zero[:, head(j)])
-
     def score(j, _):
-        keys = [
-            k_own[:, head(j)],
-            by_core(j, near_one, far_one),
-            by_core(j, far_two, near_two),
-            by_core(j, half_own, half_other),
-        ]
+        keys = [ref[:, head(j)] for ref in (k_own, k_near, k_far, k_next)]
         if with_new:
             keys.append(nk_ref[...])
         return dot_nt(head_rows(q_ref, j), jnp.concatenate(keys, axis=0))
@@ -253,12 +224,7 @@
 
     def mix(j, held):
         rounded, largest, mass = held
-        values = [
-            v_own[:, head(j)],
-            by_core(j, near_two, far_two),
-            by_core(j, far_one, near_one),
-            by_core(j, half_other, half_own),
-        ]
+        values = [ref[:, head(j)] for ref in (v_own, v_near, v_far, v_next)]
         if with_new:
             values.append(nv_ref[...])
         mixed = dot_nn(rounded, jnp.concatenate(values, axis=0))
@@ -272,21 +238,19 @@
         out_ref[TOTAL : TOTAL + STAT, :] = pack_stats(stats[0])
 
 
-def combine_kernel(own_ref, stat_ref, far_ref, near_ref, out_ref):
-    own, far, near = stat_ref[...], unpack_stats(far_ref), unpack_stats(near_ref)
-    top = jnp.maximum(jnp.maximum(own, far), near)
-    own, far, near = jnp.exp2(own - top), jnp.exp2(far - top), jnp.exp2(near - top)
-    scale = 1.0 / (own + far + near)
-    own, far, near = own * scale, far * scale, near * scale
+def merge_kernel(own_ref, stat_ref, other_ref, out_ref, *merged_stat):
+    own, other = stat_ref[...], unpack_stats(other_ref)
+    top = jnp.maximum(own, other)
+    mass = jnp.exp2(own - top) + jnp.exp2(other - top)
+    share = jnp.exp2(own - top) / mass
+    for ref in merged_stat:
+        ref[...] = top + jnp.log2(mass)
     for j in range(KVH):
         for r in range(ROWS):
             rows = slice(r * 256 + j * QR, r * 256 + (j + 1) * QR)
-            part = slice(r * QR, (r + 1) * QR)
-            out_ref[rows, :] = (
-                own_ref[rows, :] * own[part, j : j + 1]
-                + far_ref[rows, :].astype(jnp.float32) * far[part, j : j + 1]
-                + near_ref[rows, :].astype(jnp.float32) * near[part, j : j + 1]
-            ).astype(jnp.bfloat16)
+            second = other_ref[rows, :].astype(jnp.float32)
+            weight = share[r * QR : (r + 1) * QR, j : j + 1]
+            out_ref[rows, :] = (second + (own_ref[rows, :] - second) * weight).astype(out_ref.dtype)
 
 
 VMEM = pl.BlockSpec(memory_space=pltpu.VMEM)
@@ -333,27 +297,22 @@
     new_keys,
     new_values,
 ):
-    block = prefix_keys.shape
-    packed, one, two = call(
+    packed = call(
         pack_kernel,
-        in_hbm(heads_first(queries, H), prefix_keys, prefix_values, prefix_mask, row_branch.reshape(1, ROWS)),
-        [HBM] * 5,
-        (vmem((TOTAL + ROWS * EXT, HD)), vmem(block), vmem(block)),
+        in_hbm(heads_first(queries, H), prefix_mask, row_branch.reshape(1, ROWS)),
+        [HBM] * 3,
+        vmem((TOTAL + ROWS * EXT, HD)),
         [
             pltpu.VMEM(prefix_mask.shape, jnp.int32),
             pltpu.VMEM((1, ROWS), jnp.int32),
-            pltpu.SemaphoreType.DMA((5,)),
+            pltpu.SemaphoreType.DMA((3,)),
         ],
     )
-    near_one = send(one, along_x)
+    near_one = send(lax.optimization_barrier((prefix_keys, packed))[0], along_x)
     far_queries = send(packed, to_partner)
-    near_two = send(two, along_x)
-    half_own = send(near_one, along_x)
-    far_one = send(near_one, other_core)
-    far_two = send(near_two, other_core)
-
+    near_two = send(lax.optimization_barrier((prefix_values, packed))[0], along_x)
     stored = (suffix_len.reshape(1, 2), suffix_keys, suffix_values)
-    stored, packed = lax.optimization_barrier((stored, packed))
+    stored = lax.optimization_barrier((stored, packed))[0]
     stored = call(
         load_kernel,
         in_hbm(*stored),
@@ -361,25 +320,26 @@
         tuple(vmem(value.shape, value.dtype) for value in stored),
         [pltpu.SemaphoreType.DMA((3,))],
     )
-    later, _ = lax.optimization_barrier((packed, near_one))
-    near_queries = send(later, to_neighbour)
+    next_one = send(lax.optimization_barrier((near_one, stored[0]))[0], along_x)
+    next_two = send(lax.optimization_barrier((near_two, stored[0]))[0], along_x)
+    far_one = send(lax.optimization_barrier((near_one, stored[0]))[0], other_core)
+    far_two = send(lax.optimization_barrier((near_two, stored[0]))[0], other_core)
+    near_queries = send(lax.optimization_barrier((packed, near_one, stored[0]))[0], to_neighbour)
     suffix = call(suffix_kernel, (stored[0], far_queries, stored[1], stored[2]), [VMEM] * 4, PACKED)
-    half_own, _ = lax.optimization_barrier((half_own, suffix))
-    half_other = send(half_own, other_core)
     suffix = send(suffix, to_partner)
 
-    blocks = (prefix_keys, prefix_values, near_one, near_two, far_one, far_two, half_own, half_other)
+    blocks = (prefix_keys, prefix_values, near_one, near_two, far_one, far_two, next_one, next_two)
     near = call(functools.partial(prefix_kernel, False), (near_queries,) + blocks, [VMEM] * 9, PACKED)
     near = send(near, from_neighbour)
+    partial = (vmem((TOTAL, HD), jnp.float32), vmem((NQ, 128), jnp.float32))
     own, stat = call(
         functools.partial(prefix_kernel, True),
         (packed,) + blocks + (heads_first(new_keys, KVH), heads_first(new_values, KVH)),
         [VMEM] * 11,
-        (vmem((TOTAL, HD), jnp.float32), vmem((NQ, 128), jnp.float32)),
+        partial,
     )
-    merged = call(
-        combine_kernel, (own, stat, suffix, near), [VMEM] * 4, jax.ShapeDtypeStruct((TOTAL, HD), jnp.bfloat16)
-    )
+    own, stat = call(merge_kernel, (own, stat, suffix), [VMEM] * 3, partial)
+    merged = call(merge_kernel, (own, stat, near), [VMEM] * 3, jax.ShapeDtypeStruct((TOTAL, HD), jnp.bfloat16))
     merged = merged.reshape(ROWS, H, STEPS, HD).transpose(0, 2, 1, 3)
     return merged.reshape(queries.shape)
 

time: 33.8 us -> 31.5 us (0.932)
  starting transfers between devices: 16 us -> 14.9 us
  Pallas kernels: 10.1 us -> 9.39 us
  waiting for transfers between devices: 7.43 us -> 6.9 us
    ppermute x10, starting transfers between devices: 16 us -> 14.9 us  [send(): return lax.ppermute(value, AXES, pairs)]
    pallas_call x6 -> x7, Pallas kernels: 10.1 us -> 9.39 us  [call(): pl.pallas_call(kernel, out_shape=out, in_specs=specs, out_specs=jax.tree....]
    ppermute x10, waiting for transfers between devices: 7.43 us -> 6.9 us  [send(): return lax.ppermute(value, AXES, pairs)]
  transfers between devices with their start and end apart: 10 -> 10, of which waited for: 2 -> 4; matrix products, arithmetic and copies ran while one was open for 0% -> 0% of each run, Pallas kernels for 22% -> 24%
where the time goes in v3:
time: 31.5 us; the launch traced here: 31.2 us
  starting transfers between devices  14.9 us (47%)
  Pallas kernels  9.39 us (30%)
  waiting for transfers between devices  6.9 us (22%)
    ppermute x10, starting transfers between devices, send(): return lax.ppermute(value, AXES, pairs)  14.9 us
    pallas_call x7, Pallas kernels, call(): pl.pallas_call(kernel, out_shape=out, in_specs=specs, out_specs=jax.tree....  9.39 us
    ppermute x10, waiting for transfers between devices, send(): return lax.ppermute(value, AXES, pairs)  6.9 us
  transfers between devices with their start and end apart: 10, of which 4 were waited for; matrix products, arithmetic and copies ran while one was open for 0% of the time, Pallas kernels for 24%

profile of v3, /device:TPU:1, one launch (start us, length us, event | category | flops | bytes accessed | tf_op | source)
XLA Modules:
  0.0 31.2 jit_solution(5632659264594538528)
XLA Ops:
  0.0 1.0 %shard_map.100.refs_0_ = bf16[1088,128]{1,0:T(8,128)(2,1)S(1)} custom-call(bf16[1024,128]{1,0:T(8,128)(2,1)} %bitcast.24, s32[4,8]{1,0:T(4,128)} %mask_hbm.1, s32[1,4]{1,0:T(1,128)} %bitcast.25), custom_call_target="tpu_custom_call" | custom-call | flops 1 | bytes 1 | tf_op jit(solution)/shard_map/pallas_call | solution.py:272
  1.0 3.4 %collective-permute-start = (bf16[128,1024]{1,0:T(8,128)(2,1)}, bf16[128,1024]{1,0:T(8,128)(2,1)S(1)}, u32[]{:S(2)}, u32[]{:S(2)}) collective-permute-start(bf16[128,1024]{1,0:T(8,128)(2,1)} %refs_1_.4), channel_id=1, source_target_pairs={{0,32},{1,97},{2,34},{3,99},{4,36},{5,101},{6,38},{7,103},{8,40},{... | collective-permute-start | bytes 786440 | tf_op jit(solution)/shard_map/ppermute | solution.py:40
  4.4 2.9 %collective-permute-start.6 = (bf16[1088,128]{1,0:T(8,128)(2,1)S(1)}, bf16[1088,128]{1,0:T(8,128)(2,1)S(1)}, u32[]{:S(2)}, u32[]{:S(2)}) collective-permute-start(bf16[1088,128]{1,0:T(8,128)(2,1)S(1)} %shard_map.100.refs_0_), channel_id=1, source_target_pairs={{0,16},{1,17},{2,18},{3,19},{4,20},{5,21},{6,22},{7,23},{8,24},{9,... | collective-permute-start | bytes 835592 | tf_op jit(solution)/shard_map/ppermute | solution.py:40
  7.3 0.5 %collective-permute-start.1 = (bf16[128,1024]{1,0:T(8,128)(2,1)}, bf16[128,1024]{1,0:T(8,128)(2,1)S(1)}, u32[]{:S(2)}, u32[]{:S(2)}) collective-permute-start(bf16[128,1024]{1,0:T(8,128)(2,1)} %refs_2_.4), channel_id=1, source_target_pairs={{0,32},{1,97},{2,34},{3,99},{4,36},{5,101},{6,38},{7,103},{8,40},{... | collective-permute-start | bytes 786440 | tf_op jit(solution)/shard_map/ppermute | solution.py:40
  7.9 2.3 %shard_map.101 = (s32[1,2]{1,0:T(1,128)S(1)}, bf16[2,512,1024]{2,1,0:T(8,128)(2,1)S(1)}, bf16[2,512,1024]{2,1,0:T(8,128)(2,1)S(1)}) custom-call(s32[1,2]{1,0:T(1,128)} %bitcast.26, bf16[2,512,1024]{2,1,0:T(8,128)(2,1)} %refs_1_.2, bf16[2,512,1024]{2,1,0:T(8,128)(2,1)} %refs_2_.2), custom_call_target="tpu_custom_call" | custom-call | flops 1 | bytes 1 | tf_op jit(solution)/shard_map/pallas_call | solution.py:272
  10.1 0.0 collective-permute-done.refs_3_
  10.1 0.9 %collective-permute-start.8 = (bf16[1088,128]{1,0:T(8,128)(2,1)S(1)}, bf16[1088,128]{1,0:T(8,128)(2,1)S(1)}, u32[]{:S(2)}, u32[]{:S(2)}) collective-permute-start(bf16[1088,128]{1,0:T(8,128)(2,1)S(1)} %shard_map.100.refs_0_), channel_id=1, source_target_pairs={{0,128},{1,145},{2,130},{3,147},{4,132},{5,149},{6,134},{7,151},{8... | collective-permute-start | bytes 835592 | tf_op jit(solution)/shard_map/ppermute | solution.py:40
  11.0 3.1 %collective-permute-start.4 = (bf16[128,1024]{1,0:T(8,128)(2,1)S(1)}, bf16[128,1024]{1,0:T(8,128)(2,1)S(1)}, u32[]{:S(2)}, u32[]{:S(2)}) collective-permute-start(bf16[128,1024]{1,0:T(8,128)(2,1)S(1)} %collective-permute-done.refs_3_), channel_id=1, source_target_pairs={{0,32},{1,97},{2,34},{3,99},{4,36},{5,101},{6,38},{7,103},{8,40},{... | collective-permute-start | bytes 786440 | tf_op jit(solution)/shard_map/ppermute | solution.py:40
  14.1 0.0 collective-permute-start.2
  14.1 0.0 collective-permute-done.1.refs_4_
  14.1 1.0 %collective-permute-start.5 = (bf16[128,1024]{1,0:T(8,128)(2,1)S(1)}, bf16[128,1024]{1,0:T(8,128)(2,1)S(1)}, u32[]{:S(2)}, u32[]{:S(2)}) collective-permute-start(bf16[128,1024]{1,0:T(8,128)(2,1)S(1)} %collective-permute-done.1.refs_4_), channel_id=1, source_target_pairs={{0,32},{1,97},{2,34},{3,99},{4,36},{5,101},{6,38},{7,103},{8,40},{... | collective-permute-start | bytes 786440 | tf_op jit(solution)/shard_map/ppermute | solution.py:40
  15.1 0.0 collective-permute-done.6.q_ref
  15.1 0.3 collective-permute-start.3
  15.4 0.0 copy-start.1
  15.4 1.7 %shard_map.103 = bf16[1056,128]{1,0:T(8,128)(2,1)S(1)} custom-call(s32[1,2]{1,0:T(1,128)S(1)} %get-tuple-element.25.len_ref, bf16[1088,128]{1,0:T(8,128)(2,1)S(1)} %collective-permute-done.6.q_ref, bf16[2,512,1024]{2,1,0:T(8,128)(2,1)S(1)} %get-tuple-element.30.k_ref, bf16[2,512,1024]{2,1,0:T(8,128)(2,1)S(1)} %get-tuple-element.31.v_ref), custom_call_target="tpu_custom_call" | custom-call | flops 1 | bytes 1 | tf_op jit(solution)/shard_map/pallas_call | solution.py:272
  17.1 0.3 collective-permute-done.4.refs_7_
  17.4 2.4 %collective-permute-start.7 = (bf16[1056,128]{1,0:T(8,128)(2,1)S(1)}, bf16[1056,128]{1,0:T(8,128)(2,1)S(1)}, u32[]{:S(2)}, u32[]{:S(2)}) collective-permute-start(bf16[1056,128]{1,0:T(8,128)(2,1)S(1)} %shard_map.103), channel_id=1, source_target_pairs={{0,16},{1,17},{2,18},{3,19},{4,20},{5,21},{6,22},{7,23},{8,24},{9,... | collective-permute-start | bytes 811016 | tf_op jit(solution)/shard_map/ppermute | solution.py:40
  19.8 0.0 collective-permute-done.2.refs_5_
  19.8 0.4 %collective-permute-done.5.refs_8_ = bf16[128,1024]{1,0:T(8,128)(2,1)S(1)} collective-permute-done((bf16[128,1024]{1,0:T(8,128)(2,1)S(1)}, bf16[128,1024]{1,0:T(8,128)(2,1)S(1)}, u32[]{:S(2)}, u32[]{:S(2)}) %collective-permute-start.5) | collective-permute-done | bytes 262176 | tf_op jit(solution)/shard_map/ppermute | solution.py:40
  20.2 0.0 collective-permute-done.3.refs_6_
  20.2 0.0 collective-permute-done.8.refs_0_
  20.2 0.0 copy-done
  20.2 0.0 copy-done.1
  20.2 1.4 %shard_map.105 = bf16[1056,128]{1,0:T(8,128)(2,1)S(1)} custom-call(bf16[1088,128]{1,0:T(8,128)(2,1)S(1)} %collective-permute-done.8.refs_0_, bf16[128,1024]{1,0:T(8,128)(2,1)S(1)} %copy-done, bf16[128,1024]{1,0:T(8,128)(2,1)S(1)} %copy-done.1, bf16[128,1024]{1,0:T(8,128)(2,1)S(1)} %collective-permute-done.refs_3_, ...), custom_call_target="tpu_custom_call" | custom-call | flops 1 | bytes 1 | tf_op jit(solution)/shard_map/pallas_call | solution.py:272
  21.6 0.3 %collective-permute-start.9 = (bf16[1056,128]{1,0:T(8,128)(2,1)S(1)}, bf16[1056,128]{1,0:T(8,128)(2,1)S(1)}, u32[]{:S(2)}, u32[]{:S(2)}) collective-permute-start(bf16[1056,128]{1,0:T(8,128)(2,1)S(1)} %shard_map.105), channel_id=1, source_target_pairs={{0,144},{1,129},{2,146},{3,131},{4,148},{5,133},{6,150},{7,135},{8... | collective-permute-start | bytes 811016 | tf_op jit(solution)/shard_map/ppermute | solution.py:40
  22.0 0.0 copy-done.2
  22.0 0.0 copy-done.3
  22.0 1.6 %shard_map.102 = (f32[1024,128]{1,0:T(8,128)S(1)}, f32[128,128]{1,0:T(8,128)S(1)}) custom-call(bf16[1088,128]{1,0:T(8,128)(2,1)S(1)} %shard_map.100.refs_0_, bf16[128,1024]{1,0:T(8,128)(2,1)S(1)} %copy-done, bf16[128,1024]{1,0:T(8,128)(2,1)S(1)} %copy-done.1, bf16[128,1024]{1,0:T(8,128)(2,1)S(1)} %collective-permute-done.refs_3_, ...), custom_call_target="tpu_custom_call" | custom-call | flops 1 | bytes 1 | tf_op jit(solution)/shard_map/pallas_call | solution.py:272
  23.6 1.0 %collective-permute-done.7.other_ref = bf16[1056,128]{1,0:T(8,128)(2,1)S(1)} collective-permute-done((bf16[1056,128]{1,0:T(8,128)(2,1)S(1)}, bf16[1056,128]{1,0:T(8,128)(2,1)S(1)}, u32[]{:S(2)}, u32[]{:S(2)}) %collective-permute-start.7) | collective-permute-done | bytes 270368 | tf_op jit(solution)/shard_map/ppermute | solution.py:40
  24.5 0.3 %shard_map.104 = (f32[1024,128]{1,0:T(8,128)S(1)}, f32[128,128]{1,0:T(8,128)S(1)}) custom-call(f32[1024,128]{1,0:T(8,128)S(1)} %get-tuple-element.28.own_ref, f32[128,128]{1,0:T(8,128)S(1)} %get-tuple-element.29.stat_ref, bf16[1056,128]{1,0:T(8,128)(2,1)S(1)} %collective-permute-done.7.other_ref), custom_call_target="tpu_custom_call" | custom-call | flops 1 | bytes 1 | tf_op jit(solution)/shard_map/pallas_call | solution.py:272
  24.9 5.3 %collective-permute-done.9.other_ref = bf16[1056,128]{1,0:T(8,128)(2,1)S(1)} collective-permute-done((bf16[1056,128]{1,0:T(8,128)(2,1)S(1)}, bf16[1056,128]{1,0:T(8,128)(2,1)S(1)}, u32[]{:S(2)}, u32[]{:S(2)}) %collective-permute-start.9) | collective-permute-done | bytes 270368 | tf_op jit(solution)/shard_map/ppermute | solution.py:40
  30.2 1.1 %shard_map.106 = bf16[1024,128]{1,0:T(8,128)(2,1)} custom-call(f32[1024,128]{1,0:T(8,128)S(1)} %get-tuple-element.32.own_ref, f32[128,128]{1,0:T(8,128)S(1)} %get-tuple-element.33.stat_ref, bf16[1056,128]{1,0:T(8,128)(2,1)S(1)} %collective-permute-done.9.other_ref), custom_call_target="tpu_custom_call" | custom-call | flops 1 | bytes 1 | tf_op jit(solution)/shard_map/pallas_call | solution.py:272
  (3 shorter events, 0.0 us)
Async XLA Ops:
  1.0 9.1 %collective-permute-start = (bf16[128,1024]{1,0:T(8,128)(2,1)}, bf16[128,1024]{1,0:T(8,128)(2,1)S(1)}, u32[]{:S(2)}, u32[]{:S(2)}) collective-permute-start(bf16[128,1024]{1,0:T(8,128)(2,1)} %refs_1_.4), channel_id=1, source_target_pairs={{0,32},{1,97},{2,34},{3,99},{4,36},{5,101},{6,38},{7,103},{8,40},{... | collective-permute-start | bytes 786440 | tf_op jit(solution)/shard_map/ppermute | solution.py:40
  4.4 10.7 %collective-permute-start.6 = (bf16[1088,128]{1,0:T(8,128)(2,1)S(1)}, bf16[1088,128]{1,0:T(8,128)(2,1)S(1)}, u32[]{:S(2)}, u32[]{:S(2)}) collective-permute-start(bf16[1088,128]{1,0:T(8,128)(2,1)S(1)} %shard_map.100.refs_0_), channel_id=1, source_target_pairs={{0,16},{1,17},{2,18},{3,19},{4,20},{5,21},{6,22},{7,23},{8,24},{9,... | collective-permute-start | bytes 835592 | tf_op jit(solution)/shard_map/ppermute | solution.py:40
  7.3 6.8 %collective-permute-start.1 = (bf16[128,1024]{1,0:T(8,128)(2,1)}, bf16[128,1024]{1,0:T(8,128)(2,1)S(1)}, u32[]{:S(2)}, u32[]{:S(2)}) collective-permute-start(bf16[128,1024]{1,0:T(8,128)(2,1)} %refs_2_.4), channel_id=1, source_target_pairs={{0,32},{1,97},{2,34},{3,99},{4,36},{5,101},{6,38},{7,103},{8,40},{... | collective-permute-start | bytes 786440 | tf_op jit(solution)/shard_map/ppermute | solution.py:40
  10.1 10.1 %collective-permute-start.8 = (bf16[1088,128]{1,0:T(8,128)(2,1)S(1)}, bf16[1088,128]{1,0:T(8,128)(2,1)S(1)}, u32[]{:S(2)}, u32[]{:S(2)}) collective-permute-start(bf16[1088,128]{1,0:T(8,128)(2,1)S(1)} %shard_map.100.refs_0_), channel_id=1, source_target_pairs={{0,128},{1,145},{2,130},{3,147},{4,132},{5,149},{6,134},{7,151},{8... | collective-permute-start | bytes 835592 | tf_op jit(solution)/shard_map/ppermute | solution.py:40
  11.0 6.4 %collective-permute-start.4 = (bf16[128,1024]{1,0:T(8,128)(2,1)S(1)}, bf16[128,1024]{1,0:T(8,128)(2,1)S(1)}, u32[]{:S(2)}, u32[]{:S(2)}) collective-permute-start(bf16[128,1024]{1,0:T(8,128)(2,1)S(1)} %collective-permute-done.refs_3_), channel_id=1, source_target_pairs={{0,32},{1,97},{2,34},{3,99},{4,36},{5,101},{6,38},{7,103},{8,40},{... | collective-permute-start | bytes 786440 | tf_op jit(solution)/shard_map/ppermute | solution.py:40
  14.1 5.8 %collective-permute-start.2 = (bf16[128,1024]{1,0:T(8,128)(2,1)S(1)}, bf16[128,1024]{1,0:T(8,128)(2,1)S(1)}, u32[]{:S(2)}, u32[]{:S(2)}) collective-permute-start(bf16[128,1024]{1,0:T(8,128)(2,1)S(1)} %collective-permute-done.refs_3_), channel_id=1, source_target_pairs={{0,1},{1,0},{2,3},{3,2},{4,5},{5,4},{6,7},{7,6},{8,9},{9,8},{10,11... | collective-permute-start | bytes 786440 | tf_op jit(solution)/shard_map/ppermute | solution.py:40
  14.1 6.1 %collective-permute-start.5 = (bf16[128,1024]{1,0:T(8,128)(2,1)S(1)}, bf16[128,1024]{1,0:T(8,128)(2,1)S(1)}, u32[]{:S(2)}, u32[]{:S(2)}) collective-permute-start(bf16[128,1024]{1,0:T(8,128)(2,1)S(1)} %collective-permute-done.1.refs_4_), channel_id=1, source_target_pairs={{0,32},{1,97},{2,34},{3,99},{4,36},{5,101},{6,38},{7,103},{8,40},{... | collective-permute-start | bytes 786440 | tf_op jit(solution)/shard_map/ppermute | solution.py:40
  15.1 5.1 %collective-permute-start.3 = (bf16[128,1024]{1,0:T(8,128)(2,1)S(1)}, bf16[128,1024]{1,0:T(8,128)(2,1)S(1)}, u32[]{:S(2)}, u32[]{:S(2)}) collective-permute-start(bf16[128,1024]{1,0:T(8,128)(2,1)S(1)} %collective-permute-done.1.refs_4_), channel_id=1, source_target_pairs={{0,1},{1,0},{2,3},{3,2},{4,5},{5,4},{6,7},{7,6},{8,9},{9,8},{10,11... | collective-permute-start | bytes 786440 | tf_op jit(solution)/shard_map/ppermute | solution.py:40
  15.4 4.8 %copy-start = (bf16[128,1024]{1,0:T(8,128)(2,1)S(1)}, bf16[128,1024]{1,0:T(8,128)(2,1)}, u32[]{:S(2)}) copy-start(bf16[128,1024]{1,0:T(8,128)(2,1)} %refs_1_.4) | copy-start | bytes 786436
  15.4 4.8 %copy-start.1 = (bf16[128,1024]{1,0:T(8,128)(2,1)S(1)}, bf16[128,1024]{1,0:T(8,128)(2,1)}, u32[]{:S(2)}) copy-start(bf16[128,1024]{1,0:T(8,128)(2,1)} %refs_2_.4) | copy-start | bytes 786436
  17.1 4.9 %copy-start.2 = (bf16[4,4,1024]{2,1,0:T(4,128)(2,1)S(1)}, bf16[4,4,1024]{2,1,0:T(4,128)(2,1)}, u32[]{:S(2)}) copy-start(bf16[4,4,1024]{2,1,0:T(4,128)(2,1)} %param.18) | copy-start | bytes 98308
  17.1 4.9 %copy-start.3 = (bf16[4,4,1024]{2,1,0:T(4,128)(2,1)S(1)}, bf16[4,4,1024]{2,1,0:T(4,128)(2,1)}, u32[]{:S(2)}) copy-start(bf16[4,4,1024]{2,1,0:T(4,128)(2,1)} %param.19) | copy-start | bytes 98308
  17.4 7.2 %collective-permute-start.7 = (bf16[1056,128]{1,0:T(8,128)(2,1)S(1)}, bf16[1056,128]{1,0:T(8,128)(2,1)S(1)}, u32[]{:S(2)}, u32[]{:S(2)}) collective-permute-start(bf16[1056,128]{1,0:T(8,128)(2,1)S(1)} %shard_map.103), channel_id=1, source_target_pairs={{0,16},{1,17},{2,18},{3,19},{4,20},{5,21},{6,22},{7,23},{8,24},{9,... | collective-permute-start | bytes 811016 | tf_op jit(solution)/shard_map/ppermute | solution.py:40
  21.6 8.6 %collective-permute-start.9 = (bf16[1056,128]{1,0:T(8,128)(2,1)S(1)}, bf16[1056,128]{1,0:T(8,128)(2,1)S(1)}, u32[]{:S(2)}, u32[]{:S(2)}) collective-permute-start(bf16[1056,128]{1,0:T(8,128)(2,1)S(1)} %shard_map.105), channel_id=1, source_target_pairs={{0,144},{1,129},{2,146},{3,131},{4,148},{5,133},{6,150},{7,135},{8... | collective-permute-start | bytes 811016 | tf_op jit(solution)/shard_map/ppermute | solution.py:40

commit v4 on v3

--- a/solution.py
+++ b/solution.py
@@ -38,6 +38,10 @@
         for c in range(2)
     ]
     return lax.ppermute(value, AXES, pairs)
+
+
+def after(value, *others):
+    return lax.optimization_barrier((value, *others))[0]
 
 
 def to_partner(x, y, z, c):
@@ -308,27 +312,26 @@
             pltpu.SemaphoreType.DMA((3,)),
         ],
     )
-    near_one = send(lax.optimization_barrier((prefix_keys, packed))[0], along_x)
+    k_near = send(prefix_keys, along_x)
     far_queries = send(packed, to_partner)
-    near_two = send(lax.optimization_barrier((prefix_values, packed))[0], along_x)
-    stored = (suffix_len.reshape(1, 2), suffix_keys, suffix_values)
-    stored = lax.optimization_barrier((stored, packed))[0]
+    v_near = send(after(prefix_values, packed), along_x)
     stored = call(
         load_kernel,
-        in_hbm(*stored),
+        in_hbm(*after((suffix_len.reshape(1, 2), suffix_keys, suffix_values), packed)),
         [HBM] * 3,
-        tuple(vmem(value.shape, value.dtype) for value in stored),
+        (vmem((1, 2), jnp.int32), vmem(suffix_keys.shape), vmem(suffix_values.shape)),
         [pltpu.SemaphoreType.DMA((3,))],
     )
-    next_one = send(lax.optimization_barrier((near_one, stored[0]))[0], along_x)
-    next_two = send(lax.optimization_barrier((near_two, stored[0]))[0], along_x)
-    far_one = send(lax.optimization_barrier((near_one, stored[0]))[0], other_core)
-    far_two = send(lax.optimization_barrier((near_two, stored[0]))[0], other_core)
-    near_queries = send(lax.optimization_barrier((packed, near_one, stored[0]))[0], to_neighbour)
+    k_next = send(after(k_near, stored[0]), along_x)
+    v_next = send(after(v_near, stored[0]), along_x)
+    k_far = send(after(k_near, stored[0]), other_core)
+    v_far = send(after(v_near, stored[0]), other_core)
+    near_queries = send(after(packed, k_near, stored[0]), to_neighbour)
+    far_queries = after(far_queries, k_far)
     suffix = call(suffix_kernel, (stored[0], far_queries, stored[1], stored[2]), [VMEM] * 4, PACKED)
     suffix = send(suffix, to_partner)
 
-    blocks = (prefix_keys, prefix_values, near_one, near_two, far_one, far_two, next_one, next_two)
+    blocks = (prefix_keys, prefix_values, k_near, v_near, k_far, v_far, k_next, v_next)
     near = call(functools.partial(prefix_kernel, False), (near_queries,) + blocks, [VMEM] * 9, PACKED)
     near = send(near, from_neighbour)
     partial = (vmem((TOTAL, HD), jnp.float32), vmem((NQ, 128), jnp.float32))

time: 31.5 us -> 31 us (0.984)
  waiting for transfers between devices: 6.9 us -> 6.23 us
    ppermute x10, waiting for transfers between devices: 6.9 us -> 6.23 us  [send(): return lax.ppermute(value, AXES, pairs)]
    ppermute x10, starting transfers between devices: 14.9 us -> 15.2 us  [send(): return lax.ppermute(value, AXES, pairs)]
  transfers between devices with their start and end apart: 10 -> 10, of which waited for: 4 -> 3; matrix products, arithmetic and copies ran while one was open for 0% -> 0% of each run, Pallas kernels for 24% -> 27%
where the time goes in v4:
time: 31 us; the launch traced here: 30.9 us
  starting transfers between devices  15.2 us (49%)
  Pallas kernels  9.38 us (30%)
  waiting for transfers between devices  6.23 us (20%)
    ppermute x10, starting transfers between devices, send(): return lax.ppermute(value, AXES, pairs)  15.2 us
    pallas_call x7, Pallas kernels, call(): pl.pallas_call(kernel, out_shape=out, in_specs=specs, out_specs=jax.tree....  9.38 us
    ppermute x10, waiting for transfers between devices, send(): return lax.ppermute(value, AXES, pairs)  6.23 us
  transfers between devices with their start and end apart: 10, of which 3 were waited for; matrix products, arithmetic and copies ran while one was open for 0% of the time, Pallas kernels for 27%

profile of v4, /device:TPU:1, one launch (start us, length us, event | category | flops | bytes accessed | tf_op | source)
XLA Modules:
  0.0 30.9 jit_solution(14062819738248213568)
XLA Ops:
  0.0 3.3 %collective-permute-start = (bf16[128,1024]{1,0:T(8,128)(2,1)}, bf16[128,1024]{1,0:T(8,128)(2,1)S(1)}, u32[]{:S(2)}, u32[]{:S(2)}) collective-permute-start(bf16[128,1024]{1,0:T(8,128)(2,1)} %refs_1_.4), channel_id=1, source_target_pairs={{0,32},{1,97},{2,34},{3,99},{4,36},{5,101},{6,38},{7,103},{8,40},{... | collective-permute-start | bytes 786440 | tf_op jit(solution)/shard_map/ppermute | solution.py:40
  3.3 1.0 %shard_map.100.refs_0_ = bf16[1088,128]{1,0:T(8,128)(2,1)S(1)} custom-call(bf16[1024,128]{1,0:T(8,128)(2,1)} %bitcast.24, s32[4,8]{1,0:T(4,128)} %mask_hbm.1, s32[1,4]{1,0:T(1,128)} %bitcast.25), custom_call_target="tpu_custom_call" | custom-call | flops 1 | bytes 1 | tf_op jit(solution)/shard_map/pallas_call | solution.py:276
  4.3 3.0 %collective-permute-start.6 = (bf16[1088,128]{1,0:T(8,128)(2,1)S(1)}, bf16[1088,128]{1,0:T(8,128)(2,1)S(1)}, u32[]{:S(2)}, u32[]{:S(2)}) collective-permute-start(bf16[1088,128]{1,0:T(8,128)(2,1)S(1)} %shard_map.100.refs_0_), channel_id=1, source_target_pairs={{0,16},{1,17},{2,18},{3,19},{4,20},{5,21},{6,22},{7,23},{8,24},{9,... | collective-permute-start | bytes 835592 | tf_op jit(solution)/shard_map/ppermute | solution.py:40
  7.3 0.5 %collective-permute-start.1 = (bf16[128,1024]{1,0:T(8,128)(2,1)}, bf16[128,1024]{1,0:T(8,128)(2,1)S(1)}, u32[]{:S(2)}, u32[]{:S(2)}) collective-permute-start(bf16[128,1024]{1,0:T(8,128)(2,1)} %refs_2_.4), channel_id=1, source_target_pairs={{0,32},{1,97},{2,34},{3,99},{4,36},{5,101},{6,38},{7,103},{8,40},{... | collective-permute-start | bytes 786440 | tf_op jit(solution)/shard_map/ppermute | solution.py:40
  7.9 2.3 %shard_map.101 = (s32[1,2]{1,0:T(1,128)S(1)}, bf16[2,512,1024]{2,1,0:T(8,128)(2,1)S(1)}, bf16[2,512,1024]{2,1,0:T(8,128)(2,1)S(1)}) custom-call(s32[1,2]{1,0:T(1,128)} %bitcast.26, bf16[2,512,1024]{2,1,0:T(8,128)(2,1)} %refs_1_.2, bf16[2,512,1024]{2,1,0:T(8,128)(2,1)} %refs_2_.2), custom_call_target="tpu_custom_call" | custom-call | flops 1 | bytes 1 | tf_op jit(solution)/shard_map/pallas_call | solution.py:276
  10.1 0.0 collective-permute-done.refs_3_
  10.2 0.9 %collective-permute-start.8 = (bf16[1088,128]{1,0:T(8,128)(2,1)S(1)}, bf16[1088,128]{1,0:T(8,128)(2,1)S(1)}, u32[]{:S(2)}, u32[]{:S(2)}) collective-permute-start(bf16[1088,128]{1,0:T(8,128)(2,1)S(1)} %shard_map.100.refs_0_), channel_id=1, source_target_pairs={{0,128},{1,145},{2,130},{3,147},{4,132},{5,149},{6,134},{7,151},{8... | collective-permute-start | bytes 835592 | tf_op jit(solution)/shard_map/ppermute | solution.py:40
  11.0 0.8 %collective-permute-start.2 = (bf16[128,1024]{1,0:T(8,128)(2,1)S(1)}, bf16[128,1024]{1,0:T(8,128)(2,1)S(1)}, u32[]{:S(2)}, u32[]{:S(2)}) collective-permute-start(bf16[128,1024]{1,0:T(8,128)(2,1)S(1)} %collective-permute-done.refs_3_), channel_id=1, source_target_pairs={{0,1},{1,0},{2,3},{3,2},{4,5},{5,4},{6,7},{7,6},{8,9},{9,8},{10,11... | collective-permute-start | bytes 786440 | tf_op jit(solution)/shard_map/ppermute | solution.py:40
  11.8 1.5 %collective-permute-start.4 = (bf16[128,1024]{1,0:T(8,128)(2,1)S(1)}, bf16[128,1024]{1,0:T(8,128)(2,1)S(1)}, u32[]{:S(2)}, u32[]{:S(2)}) collective-permute-start(bf16[128,1024]{1,0:T(8,128)(2,1)S(1)} %collective-permute-done.refs_3_), channel_id=1, source_target_pairs={{0,32},{1,97},{2,34},{3,99},{4,36},{5,101},{6,38},{7,103},{8,40},{... | collective-permute-start | bytes 786440 | tf_op jit(solution)/shard_map/ppermute | solution.py:40
  13.3 0.0 collective-permute-done.1.refs_4_
  13.3 1.5 %collective-permute-start.5 = (bf16[128,1024]{1,0:T(8,128)(2,1)S(1)}, bf16[128,1024]{1,0:T(8,128)(2,1)S(1)}, u32[]{:S(2)}, u32[]{:S(2)}) collective-permute-start(bf16[128,1024]{1,0:T(8,128)(2,1)S(1)} %collective-permute-done.1.refs_4_), channel_id=1, source_target_pairs={{0,32},{1,97},{2,34},{3,99},{4,36},{5,101},{6,38},{7,103},{8,40},{... | collective-permute-start | bytes 786440 | tf_op jit(solution)/shard_map/ppermute | solution.py:40
  14.8 0.0 collective-permute-done.6.q_ref
  14.8 0.6 %collective-permute-start.3 = (bf16[128,1024]{1,0:T(8,128)(2,1)S(1)}, bf16[128,1024]{1,0:T(8,128)(2,1)S(1)}, u32[]{:S(2)}, u32[]{:S(2)}) collective-permute-start(bf16[128,1024]{1,0:T(8,128)(2,1)S(1)} %collective-permute-done.1.refs_4_), channel_id=1, source_target_pairs={{0,1},{1,0},{2,3},{3,2},{4,5},{5,4},{6,7},{7,6},{8,9},{9,8},{10,11... | collective-permute-start | bytes 786440 | tf_op jit(solution)/shard_map/ppermute | solution.py:40
  15.4 0.0 collective-permute-done.2.refs_5_
  15.4 0.0 copy-start
  15.4 1.7 %shard_map.103 = bf16[1056,128]{1,0:T(8,128)(2,1)S(1)} custom-call(s32[1,2]{1,0:T(1,128)S(1)} %get-tuple-element.24.len_ref, bf16[1088,128]{1,0:T(8,128)(2,1)S(1)} %collective-permute-done.6.q_ref, bf16[2,512,1024]{2,1,0:T(8,128)(2,1)S(1)} %get-tuple-element.30.k_ref, bf16[2,512,1024]{2,1,0:T(8,128)(2,1)S(1)} %get-tuple-element.31.v_ref), custom_call_target="tpu_custom_call" | custom-call | flops 1 | bytes 1 | tf_op jit(solution)/shard_map/pallas_call | solution.py:276
  17.1 2.7 %collective-permute-start.7 = (bf16[1056,128]{1,0:T(8,128)(2,1)S(1)}, bf16[1056,128]{1,0:T(8,128)(2,1)S(1)}, u32[]{:S(2)}, u32[]{:S(2)}) collective-permute-start(bf16[1056,128]{1,0:T(8,128)(2,1)S(1)} %shard_map.103), channel_id=1, source_target_pairs={{0,16},{1,17},{2,18},{3,19},{4,20},{5,21},{6,22},{7,23},{8,24},{9,... | collective-permute-start | bytes 811016 | tf_op jit(solution)/shard_map/ppermute | solution.py:40
  19.8 0.0 collective-permute-done.4.refs_7_
  19.9 0.3 collective-permute-done.5.refs_8_
  20.1 0.0 collective-permute-done.3.refs_6_
  20.2 0.0 collective-permute-done.8.refs_0_
  20.2 0.0 copy-done
  20.2 0.0 copy-done.1
  20.2 1.4 %shard_map.105 = bf16[1056,128]{1,0:T(8,128)(2,1)S(1)} custom-call(bf16[1088,128]{1,0:T(8,128)(2,1)S(1)} %collective-permute-done.8.refs_0_, bf16[128,1024]{1,0:T(8,128)(2,1)S(1)} %copy-done, bf16[128,1024]{1,0:T(8,128)(2,1)S(1)} %copy-done.1, bf16[128,1024]{1,0:T(8,128)(2,1)S(1)} %collective-permute-done.refs_3_, ...), custom_call_target="tpu_custom_call" | custom-call | flops 1 | bytes 1 | tf_op jit(solution)/shard_map/pallas_call | solution.py:276
  21.5 0.4 %collective-permute-start.9 = (bf16[1056,128]{1,0:T(8,128)(2,1)S(1)}, bf16[1056,128]{1,0:T(8,128)(2,1)S(1)}, u32[]{:S(2)}, u32[]{:S(2)}) collective-permute-start(bf16[1056,128]{1,0:T(8,128)(2,1)S(1)} %shard_map.105), channel_id=1, source_target_pairs={{0,144},{1,129},{2,146},{3,131},{4,148},{5,133},{6,150},{7,135},{8... | collective-permute-start | bytes 811016 | tf_op jit(solution)/shard_map/ppermute | solution.py:40
  21.9 0.0 copy-done.2
  21.9 0.0 copy-done.3
  21.9 1.6 %shard_map.102 = (f32[1024,128]{1,0:T(8,128)S(1)}, f32[128,128]{1,0:T(8,128)S(1)}) custom-call(bf16[1088,128]{1,0:T(8,128)(2,1)S(1)} %shard_map.100.refs_0_, bf16[128,1024]{1,0:T(8,128)(2,1)S(1)} %copy-done, bf16[128,1024]{1,0:T(8,128)(2,1)S(1)} %copy-done.1, bf16[128,1024]{1,0:T(8,128)(2,1)S(1)} %collective-permute-done.refs_3_, ...), custom_call_target="tpu_custom_call" | custom-call | flops 1 | bytes 1 | tf_op jit(solution)/shard_map/pallas_call | solution.py:276
  23.6 3.2 %collective-permute-done.7.other_ref = bf16[1056,128]{1,0:T(8,128)(2,1)S(1)} collective-permute-done((bf16[1056,128]{1,0:T(8,128)(2,1)S(1)}, bf16[1056,128]{1,0:T(8,128)(2,1)S(1)}, u32[]{:S(2)}, u32[]{:S(2)}) %collective-permute-start.7) | collective-permute-done | bytes 270368 | tf_op jit(solution)/shard_map/ppermute | solution.py:40
  26.8 0.3 %shard_map.104 = (f32[1024,128]{1,0:T(8,128)S(1)}, f32[128,128]{1,0:T(8,128)S(1)}) custom-call(f32[1024,128]{1,0:T(8,128)S(1)} %get-tuple-element.27.own_ref, f32[128,128]{1,0:T(8,128)S(1)} %get-tuple-element.28.stat_ref, bf16[1056,128]{1,0:T(8,128)(2,1)S(1)} %collective-permute-done.7.other_ref), custom_call_target="tpu_custom_call" | custom-call | flops 1 | bytes 1 | tf_op jit(solution)/shard_map/pallas_call | solution.py:276
  27.2 2.7 %collective-permute-done.9.other_ref = bf16[1056,128]{1,0:T(8,128)(2,1)S(1)} collective-permute-done((bf16[1056,128]{1,0:T(8,128)(2,1)S(1)}, bf16[1056,128]{1,0:T(8,128)(2,1)S(1)}, u32[]{:S(2)}, u32[]{:S(2)}) %collective-permute-start.9) | collective-permute-done | bytes 270368 | tf_op jit(solution)/shard_map/ppermute | solution.py:40
  29.8 1.1 %shard_map.106 = bf16[1024,128]{1,0:T(8,128)(2,1)} custom-call(f32[1024,128]{1,0:T(8,128)S(1)} %get-tuple-element.32.own_ref, f32[128,128]{1,0:T(8,128)S(1)} %get-tuple-element.33.stat_ref, bf16[1056,128]{1,0:T(8,128)(2,1)S(1)} %collective-permute-done.9.other_ref), custom_call_target="tpu_custom_call" | custom-call | flops 1 | bytes 1 | tf_op jit(solution)/shard_map/pallas_call | solution.py:276
  (3 shorter events, 0.0 us)
Async XLA Ops:
  0.0 10.1 %collective-permute-start = (bf16[128,1024]{1,0:T(8,128)(2,1)}, bf16[128,1024]{1,0:T(8,128)(2,1)S(1)}, u32[]{:S(2)}, u32[]{:S(2)}) collective-permute-start(bf16[128,1024]{1,0:T(8,128)(2,1)} %refs_1_.4), channel_id=1, source_target_pairs={{0,32},{1,97},{2,34},{3,99},{4,36},{5,101},{6,38},{7,103},{8,40},{... | collective-permute-start | bytes 786440 | tf_op jit(solution)/shard_map/ppermute | solution.py:40
  4.3 10.5 %collective-permute-start.6 = (bf16[1088,128]{1,0:T(8,128)(2,1)S(1)}, bf16[1088,128]{1,0:T(8,128)(2,1)S(1)}, u32[]{:S(2)}, u32[]{:S(2)}) collective-permute-start(bf16[1088,128]{1,0:T(8,128)(2,1)S(1)} %shard_map.100.refs_0_), channel_id=1, source_target_pairs={{0,16},{1,17},{2,18},{3,19},{4,20},{5,21},{6,22},{7,23},{8,24},{9,... | collective-permute-start | bytes 835592 | tf_op jit(solution)/shard_map/ppermute | solution.py:40
  7.3 6.0 %collective-permute-start.1 = (bf16[128,1024]{1,0:T(8,128)(2,1)}, bf16[128,1024]{1,0:T(8,128)(2,1)S(1)}, u32[]{:S(2)}, u32[]{:S(2)}) collective-permute-start(bf16[128,1024]{1,0:T(8,128)(2,1)} %refs_2_.4), channel_id=1, source_target_pairs={{0,32},{1,97},{2,34},{3,99},{4,36},{5,101},{6,38},{7,103},{8,40},{... | collective-permute-start | bytes 786440 | tf_op jit(solution)/shard_map/ppermute | solution.py:40
  10.2 10.0 %collective-permute-start.8 = (bf16[1088,128]{1,0:T(8,128)(2,1)S(1)}, bf16[1088,128]{1,0:T(8,128)(2,1)S(1)}, u32[]{:S(2)}, u32[]{:S(2)}) collective-permute-start(bf16[1088,128]{1,0:T(8,128)(2,1)S(1)} %shard_map.100.refs_0_), channel_id=1, source_target_pairs={{0,128},{1,145},{2,130},{3,147},{4,132},{5,149},{6,134},{7,151},{8... | collective-permute-start | bytes 835592 | tf_op jit(solution)/shard_map/ppermute | solution.py:40
  11.0 4.4 %collective-permute-start.2 = (bf16[128,1024]{1,0:T(8,128)(2,1)S(1)}, bf16[128,1024]{1,0:T(8,128)(2,1)S(1)}, u32[]{:S(2)}, u32[]{:S(2)}) collective-permute-start(bf16[128,1024]{1,0:T(8,128)(2,1)S(1)} %collective-permute-done.refs_3_), channel_id=1, source_target_pairs={{0,1},{1,0},{2,3},{3,2},{4,5},{5,4},{6,7},{7,6},{8,9},{9,8},{10,11... | collective-permute-start | bytes 786440 | tf_op jit(solution)/shard_map/ppermute | solution.py:40
  11.8 8.0 %collective-permute-start.4 = (bf16[128,1024]{1,0:T(8,128)(2,1)S(1)}, bf16[128,1024]{1,0:T(8,128)(2,1)S(1)}, u32[]{:S(2)}, u32[]{:S(2)}) collective-permute-start(bf16[128,1024]{1,0:T(8,128)(2,1)S(1)} %collective-permute-done.refs_3_), channel_id=1, source_target_pairs={{0,32},{1,97},{2,34},{3,99},{4,36},{5,101},{6,38},{7,103},{8,40},{... | collective-permute-start | bytes 786440 | tf_op jit(solution)/shard_map/ppermute | solution.py:40
  13.3 6.9 %collective-permute-start.5 = (bf16[128,1024]{1,0:T(8,128)(2,1)S(1)}, bf16[128,1024]{1,0:T(8,128)(2,1)S(1)}, u32[]{:S(2)}, u32[]{:S(2)}) collective-permute-start(bf16[128,1024]{1,0:T(8,128)(2,1)S(1)} %collective-permute-done.1.refs_4_), channel_id=1, source_target_pairs={{0,32},{1,97},{2,34},{3,99},{4,36},{5,101},{6,38},{7,103},{8,40},{... | collective-permute-start | bytes 786440 | tf_op jit(solution)/shard_map/ppermute | solution.py:40
  14.8 5.3 %collective-permute-start.3 = (bf16[128,1024]{1,0:T(8,128)(2,1)S(1)}, bf16[128,1024]{1,0:T(8,128)(2,1)S(1)}, u32[]{:S(2)}, u32[]{:S(2)}) collective-permute-start(bf16[128,1024]{1,0:T(8,128)(2,1)S(1)} %collective-permute-done.1.refs_4_), channel_id=1, source_target_pairs={{0,1},{1,0},{2,3},{3,2},{4,5},{5,4},{6,7},{7,6},{8,9},{9,8},{10,11... | collective-permute-start | bytes 786440 | tf_op jit(solution)/shard_map/ppermute | solution.py:40
  15.4 4.8 %copy-start = (bf16[128,1024]{1,0:T(8,128)(2,1)S(1)}, bf16[128,1024]{1,0:T(8,128)(2,1)}, u32[]{:S(2)}) copy-start(bf16[128,1024]{1,0:T(8,128)(2,1)} %refs_1_.4) | copy-start | bytes 786436
  15.4 4.8 %copy-start.1 = (bf16[128,1024]{1,0:T(8,128)(2,1)S(1)}, bf16[128,1024]{1,0:T(8,128)(2,1)}, u32[]{:S(2)}) copy-start(bf16[128,1024]{1,0:T(8,128)(2,1)} %refs_2_.4) | copy-start | bytes 786436
  17.1 4.8 %copy-start.2 = (bf16[4,4,1024]{2,1,0:T(4,128)(2,1)S(1)}, bf16[4,4,1024]{2,1,0:T(4,128)(2,1)}, u32[]{:S(2)}) copy-start(bf16[4,4,1024]{2,1,0:T(4,128)(2,1)} %param.18) | copy-start | bytes 98308
  17.1 4.8 %copy-start.3 = (bf16[4,4,1024]{2,1,0:T(4,128)(2,1)S(1)}, bf16[4,4,1024]{2,1,0:T(4,128)(2,1)}, u32[]{:S(2)}) copy-start(bf16[4,4,1024]{2,1,0:T(4,128)(2,1)} %param.19) | copy-start | bytes 98308
  17.1 9.7 %collective-permute-start.7 = (bf16[1056,128]{1,0:T(8,128)(2,1)S(1)}, bf16[1056,128]{1,0:T(8,128)(2,1)S(1)}, u32[]{:S(2)}, u32[]{:S(2)}) collective-permute-start(bf16[1056,128]{1,0:T(8,128)(2,1)S(1)} %shard_map.103), channel_id=1, source_target_pairs={{0,16},{1,17},{2,18},{3,19},{4,20},{5,21},{6,22},{7,23},{8,24},{9,... | collective-permute-start | bytes 811016 | tf_op jit(solution)/shard_map/ppermute | solution.py:40
  21.5 8.3 %collective-permute-start.9 = (bf16[1056,128]{1,0:T(8,128)(2,1)S(1)}, bf16[1056,128]{1,0:T(8,128)(2,1)S(1)}, u32[]{:S(2)}, u32[]{:S(2)}) collective-permute-start(bf16[1056,128]{1,0:T(8,128)(2,1)S(1)} %shard_map.105), channel_id=1, source_target_pairs={{0,144},{1,129},{2,146},{3,131},{4,148},{5,133},{6,150},{7,135},{8... | collective-permute-start | bytes 811016 | tf_op jit(solution)/shard_map/ppermute | solution.py:40

commit v5 on v4

--- a/solution.py
+++ b/solution.py
@@ -77,14 +77,11 @@
 
 
 def ext_column(q_ref, lane):
-    ext = q_ref[TOTAL : TOTAL + ROWS * EXT, :].astype(jnp.float32)
+    ext = q_ref[TOTAL : TOTAL + EXT, :].astype(jnp.float32)
     lanes = lax.broadcasted_iota(jnp.int32, ext.shape, 1)
     column = jnp.sum(jnp.where(lanes == lane, ext, 0.0), axis=1, keepdims=True)
-    pieces = []
-    for r in range(ROWS):
-        piece = column[r * EXT : (r + 1) * EXT, :]
-        pieces += [piece, piece]
-    return jnp.concatenate(pieces, axis=0)
+    each = EXT // ROWS
+    return jnp.concatenate([jnp.broadcast_to(column[r * each : r * each + 1, :], (QR, 1)) for r in range(ROWS)], axis=0)
 
 
 def pack_stats(stat):
@@ -149,9 +146,8 @@
     for r in range(ROWS):
         extra = jnp.where((lanes == KVH) & (rows == r), branch_ref[:, r : r + 1], extra)
     extra = extra.astype(jnp.float32)
-    for r in range(ROWS):
-        tile = jnp.broadcast_to(extra[r : r + 1, :], (EXT, HD)).astype(jnp.bfloat16)
-        packed_ref[TOTAL + r * EXT : TOTAL + (r + 1) * EXT, :] = tile
+    tile = [jnp.broadcast_to(extra[r : r + 1, :], (EXT // ROWS, HD)) for r in range(ROWS)]
+    packed_ref[TOTAL : TOTAL + EXT, :] = jnp.concatenate(tile, axis=0).astype(jnp.bfloat16)
     queries.wait()
 
 
@@ -305,7 +301,7 @@
         pack_kernel,
         in_hbm(heads_first(queries, H), prefix_mask, row_branch.reshape(1, ROWS)),
         [HBM] * 3,
-        vmem((TOTAL + ROWS * EXT, HD)),
+        vmem((TOTAL + EXT, HD)),
         [
             pltpu.VMEM(prefix_mask.shape, jnp.int32),
             pltpu.VMEM((1, ROWS), jnp.int32),

time: 31 us -> 30.9 us (level)
  no operation moved by 1% of the time
where the time goes in v5:
time: 30.9 us; the launch traced here: 30.8 us
  starting transfers between devices  14.9 us (48%)
  Pallas kernels  9.33 us (30%)
  waiting for transfers between devices  6.5 us (21%)
    ppermute x10, starting transfers between devices, send(): return lax.ppermute(value, AXES, pairs)  14.9 us
    pallas_call x7, Pallas kernels, call(): pl.pallas_call(kernel, out_shape=out, in_specs=specs, out_specs=jax.tree....  9.33 us
    ppermute x10, waiting for transfers between devices, send(): return lax.ppermute(value, AXES, pairs)  6.5 us
  transfers between devices with their start and end apart: 10, of which 3 were waited for; matrix products, arithmetic and copies ran while one was open for 0% of the time, Pallas kernels for 27%

profile of v5, /device:TPU:1, one launch (start us, length us, event | category | flops | bytes accessed | tf_op | source)
XLA Modules:
  0.0 30.8 jit_solution(12314265886923137672)
XLA Ops:
  0.0 3.3 %collective-permute-start = (bf16[128,1024]{1,0:T(8,128)(2,1)}, bf16[128,1024]{1,0:T(8,128)(2,1)S(1)}, u32[]{:S(2)}, u32[]{:S(2)}) collective-permute-start(bf16[128,1024]{1,0:T(8,128)(2,1)} %refs_1_.4), channel_id=1, source_target_pairs={{0,32},{1,97},{2,34},{3,99},{4,36},{5,101},{6,38},{7,103},{8,40},{... | collective-permute-start | bytes 786440 | tf_op jit(solution)/shard_map/ppermute | solution.py:40
  3.3 1.0 %shard_map.100.refs_0_ = bf16[1040,128]{1,0:T(8,128)(2,1)S(1)} custom-call(bf16[1024,128]{1,0:T(8,128)(2,1)} %bitcast.24, s32[4,8]{1,0:T(4,128)} %mask_hbm.1, s32[1,4]{1,0:T(1,128)} %bitcast.25), custom_call_target="tpu_custom_call" | custom-call | flops 1 | bytes 1 | tf_op jit(solution)/shard_map/pallas_call | solution.py:272
  4.3 3.0 %collective-permute-start.6 = (bf16[1040,128]{1,0:T(8,128)(2,1)S(1)}, bf16[1040,128]{1,0:T(8,128)(2,1)S(1)}, u32[]{:S(2)}, u32[]{:S(2)}) collective-permute-start(bf16[1040,128]{1,0:T(8,128)(2,1)S(1)} %shard_map.100.refs_0_), channel_id=1, source_target_pairs={{0,16},{1,17},{2,18},{3,19},{4,20},{5,21},{6,22},{7,23},{8,24},{9,... | collective-permute-start | bytes 798728 | tf_op jit(solution)/shard_map/ppermute | solution.py:40
  7.3 0.5 %collective-permute-start.1 = (bf16[128,1024]{1,0:T(8,128)(2,1)}, bf16[128,1024]{1,0:T(8,128)(2,1)S(1)}, u32[]{:S(2)}, u32[]{:S(2)}) collective-permute-start(bf16[128,1024]{1,0:T(8,128)(2,1)} %refs_2_.4), channel_id=1, source_target_pairs={{0,32},{1,97},{2,34},{3,99},{4,36},{5,101},{6,38},{7,103},{8,40},{... | collective-permute-start | bytes 786440 | tf_op jit(solution)/shard_map/ppermute | solution.py:40
  7.9 2.3 %shard_map.101 = (s32[1,2]{1,0:T(1,128)S(1)}, bf16[2,512,1024]{2,1,0:T(8,128)(2,1)S(1)}, bf16[2,512,1024]{2,1,0:T(8,128)(2,1)S(1)}) custom-call(s32[1,2]{1,0:T(1,128)} %bitcast.26, bf16[2,512,1024]{2,1,0:T(8,128)(2,1)} %refs_1_.2, bf16[2,512,1024]{2,1,0:T(8,128)(2,1)} %refs_2_.2), custom_call_target="tpu_custom_call" | custom-call | flops 1 | bytes 1 | tf_op jit(solution)/shard_map/pallas_call | solution.py:272
  10.1 0.0 collective-permute-done.refs_3_
  10.2 0.9 %collective-permute-start.8 = (bf16[1040,128]{1,0:T(8,128)(2,1)S(1)}, bf16[1040,128]{1,0:T(8,128)(2,1)S(1)}, u32[]{:S(2)}, u32[]{:S(2)}) collective-permute-start(bf16[1040,128]{1,0:T(8,128)(2,1)S(1)} %shard_map.100.refs_0_), channel_id=1, source_target_pairs={{0,128},{1,145},{2,130},{3,147},{4,132},{5,149},{6,134},{7,151},{8... | collective-permute-start | bytes 798728 | tf_op jit(solution)/shard_map/ppermute | solution.py:40
  11.0 0.8 %collective-permute-start.2 = (bf16[128,1024]{1,0:T(8,128)(2,1)S(1)}, bf16[128,1024]{1,0:T(8,128)(2,1)S(1)}, u32[]{:S(2)}, u32[]{:S(2)}) collective-permute-start(bf16[128,1024]{1,0:T(8,128)(2,1)S(1)} %collective-permute-done.refs_3_), channel_id=1, source_target_pairs={{0,1},{1,0},{2,3},{3,2},{4,5},{5,4},{6,7},{7,6},{8,9},{9,8},{10,11... | collective-permute-start | bytes 786440 | tf_op jit(solution)/shard_map/ppermute | solution.py:40
  11.8 1.5 %collective-permute-start.4 = (bf16[128,1024]{1,0:T(8,128)(2,1)S(1)}, bf16[128,1024]{1,0:T(8,128)(2,1)S(1)}, u32[]{:S(2)}, u32[]{:S(2)}) collective-permute-start(bf16[128,1024]{1,0:T(8,128)(2,1)S(1)} %collective-permute-done.refs_3_), channel_id=1, source_target_pairs={{0,32},{1,97},{2,34},{3,99},{4,36},{5,101},{6,38},{7,103},{8,40},{... | collective-permute-start | bytes 786440 | tf_op jit(solution)/shard_map/ppermute | solution.py:40
  13.3 0.0 collective-permute-done.1.refs_4_
  13.3 1.5 %collective-permute-start.5 = (bf16[128,1024]{1,0:T(8,128)(2,1)S(1)}, bf16[128,1024]{1,0:T(8,128)(2,1)S(1)}, u32[]{:S(2)}, u32[]{:S(2)}) collective-permute-start(bf16[128,1024]{1,0:T(8,128)(2,1)S(1)} %collective-permute-done.1.refs_4_), channel_id=1, source_target_pairs={{0,32},{1,97},{2,34},{3,99},{4,36},{5,101},{6,38},{7,103},{8,40},{... | collective-permute-start | bytes 786440 | tf_op jit(solution)/shard_map/ppermute | solution.py:40
  14.8 0.0 collective-permute-done.6.q_ref
  14.8 0.6 %collective-permute-start.3 = (bf16[128,1024]{1,0:T(8,128)(2,1)S(1)}, bf16[128,1024]{1,0:T(8,128)(2,1)S(1)}, u32[]{:S(2)}, u32[]{:S(2)}) collective-permute-start(bf16[128,1024]{1,0:T(8,128)(2,1)S(1)} %collective-permute-done.1.refs_4_), channel_id=1, source_target_pairs={{0,1},{1,0},{2,3},{3,2},{4,5},{5,4},{6,7},{7,6},{8,9},{9,8},{10,11... | collective-permute-start | bytes 786440 | tf_op jit(solution)/shard_map/ppermute | solution.py:40
  15.4 0.0 collective-permute-done.2.refs_5_
  15.4 0.0 copy-start.1
  15.4 1.7 %shard_map.103 = bf16[1056,128]{1,0:T(8,128)(2,1)S(1)} custom-call(s32[1,2]{1,0:T(1,128)S(1)} %get-tuple-element.24.len_ref, bf16[1040,128]{1,0:T(8,128)(2,1)S(1)} %collective-permute-done.6.q_ref, bf16[2,512,1024]{2,1,0:T(8,128)(2,1)S(1)} %get-tuple-element.30.k_ref, bf16[2,512,1024]{2,1,0:T(8,128)(2,1)S(1)} %get-tuple-element.31.v_ref), custom_call_target="tpu_custom_call" | custom-call | flops 1 | bytes 1 | tf_op jit(solution)/shard_map/pallas_call | solution.py:272
  17.1 2.5 %collective-permute-start.7 = (bf16[1056,128]{1,0:T(8,128)(2,1)S(1)}, bf16[1056,128]{1,0:T(8,128)(2,1)S(1)}, u32[]{:S(2)}, u32[]{:S(2)}) collective-permute-start(bf16[1056,128]{1,0:T(8,128)(2,1)S(1)} %shard_map.103), channel_id=1, source_target_pairs={{0,16},{1,17},{2,18},{3,19},{4,20},{5,21},{6,22},{7,23},{8,24},{9,... | collective-permute-start | bytes 811016 | tf_op jit(solution)/shard_map/ppermute | solution.py:40
  19.6 0.0 collective-permute-done.4.refs_7_
  19.6 0.6 %collective-permute-done.5.refs_8_ = bf16[128,1024]{1,0:T(8,128)(2,1)S(1)} collective-permute-done((bf16[128,1024]{1,0:T(8,128)(2,1)S(1)}, bf16[128,1024]{1,0:T(8,128)(2,1)S(1)}, u32[]{:S(2)}, u32[]{:S(2)}) %collective-permute-start.5) | collective-permute-done | bytes 262176 | tf_op jit(solution)/shard_map/ppermute | solution.py:40
  20.1 0.0 collective-permute-done.3.refs_6_
  20.2 0.0 collective-permute-done.8.refs_0_
  20.2 0.0 copy-done
  20.2 0.0 copy-done.1
  20.2 1.4 %shard_map.105 = bf16[1056,128]{1,0:T(8,128)(2,1)S(1)} custom-call(bf16[1040,128]{1,0:T(8,128)(2,1)S(1)} %collective-permute-done.8.refs_0_, bf16[128,1024]{1,0:T(8,128)(2,1)S(1)} %copy-done, bf16[128,1024]{1,0:T(8,128)(2,1)S(1)} %copy-done.1, bf16[128,1024]{1,0:T(8,128)(2,1)S(1)} %collective-permute-done.refs_3_, ...), custom_call_target="tpu_custom_call" | custom-call | flops 1 | bytes 1 | tf_op jit(solution)/shard_map/pallas_call | solution.py:272
  21.5 0.4 %collective-permute-start.9 = (bf16[1056,128]{1,0:T(8,128)(2,1)S(1)}, bf16[1056,128]{1,0:T(8,128)(2,1)S(1)}, u32[]{:S(2)}, u32[]{:S(2)}) collective-permute-start(bf16[1056,128]{1,0:T(8,128)(2,1)S(1)} %shard_map.105), channel_id=1, source_target_pairs={{0,144},{1,129},{2,146},{3,131},{4,148},{5,133},{6,150},{7,135},{8... | collective-permute-start | bytes 811016 | tf_op jit(solution)/shard_map/ppermute | solution.py:40
  21.9 0.0 copy-done.2
  21.9 0.0 copy-done.3
  21.9 1.6 %shard_map.102 = (f32[1024,128]{1,0:T(8,128)S(1)}, f32[128,128]{1,0:T(8,128)S(1)}) custom-call(bf16[1040,128]{1,0:T(8,128)(2,1)S(1)} %shard_map.100.refs_0_, bf16[128,1024]{1,0:T(8,128)(2,1)S(1)} %copy-done, bf16[128,1024]{1,0:T(8,128)(2,1)S(1)} %copy-done.1, bf16[128,1024]{1,0:T(8,128)(2,1)S(1)} %collective-permute-done.refs_3_, ...), custom_call_target="tpu_custom_call" | custom-call | flops 1 | bytes 1 | tf_op jit(solution)/shard_map/pallas_call | solution.py:272
  23.5 3.2 %collective-permute-done.7.other_ref = bf16[1056,128]{1,0:T(8,128)(2,1)S(1)} collective-permute-done((bf16[1056,128]{1,0:T(8,128)(2,1)S(1)}, bf16[1056,128]{1,0:T(8,128)(2,1)S(1)}, u32[]{:S(2)}, u32[]{:S(2)}) %collective-permute-start.7) | collective-permute-done | bytes 270368 | tf_op jit(solution)/shard_map/ppermute | solution.py:40
  26.8 0.3 %shard_map.104 = (f32[1024,128]{1,0:T(8,128)S(1)}, f32[128,128]{1,0:T(8,128)S(1)}) custom-call(f32[1024,128]{1,0:T(8,128)S(1)} %get-tuple-element.27.own_ref, f32[128,128]{1,0:T(8,128)S(1)} %get-tuple-element.28.stat_ref, bf16[1056,128]{1,0:T(8,128)(2,1)S(1)} %collective-permute-done.7.other_ref), custom_call_target="tpu_custom_call" | custom-call | flops 1 | bytes 1 | tf_op jit(solution)/shard_map/pallas_call | solution.py:272
  27.1 2.7 %collective-permute-done.9.other_ref = bf16[1056,128]{1,0:T(8,128)(2,1)S(1)} collective-permute-done((bf16[1056,128]{1,0:T(8,128)(2,1)S(1)}, bf16[1056,128]{1,0:T(8,128)(2,1)S(1)}, u32[]{:S(2)}, u32[]{:S(2)}) %collective-permute-start.9) | collective-permute-done | bytes 270368 | tf_op jit(solution)/shard_map/ppermute | solution.py:40
  29.8 1.1 %shard_map.106 = bf16[1024,128]{1,0:T(8,128)(2,1)} custom-call(f32[1024,128]{1,0:T(8,128)S(1)} %get-tuple-element.32.own_ref, f32[128,128]{1,0:T(8,128)S(1)} %get-tuple-element.33.stat_ref, bf16[1056,128]{1,0:T(8,128)(2,1)S(1)} %collective-permute-done.9.other_ref), custom_call_target="tpu_custom_call" | custom-call | flops 1 | bytes 1 | tf_op jit(solution)/shard_map/pallas_call | solution.py:272
  (3 shorter events, 0.0 us)
Async XLA Ops:
  0.0 10.1 %collective-permute-start = (bf16[128,1024]{1,0:T(8,128)(2,1)}, bf16[128,1024]{1,0:T(8,128)(2,1)S(1)}, u32[]{:S(2)}, u32[]{:S(2)}) collective-permute-start(bf16[128,1024]{1,0:T(8,128)(2,1)} %refs_1_.4), channel_id=1, source_target_pairs={{0,32},{1,97},{2,34},{3,99},{4,36},{5,101},{6,38},{7,103},{8,40},{... | collective-permute-start | bytes 786440 | tf_op jit(solution)/shard_map/ppermute | solution.py:40
  4.3 10.5 %collective-permute-start.6 = (bf16[1040,128]{1,0:T(8,128)(2,1)S(1)}, bf16[1040,128]{1,0:T(8,128)(2,1)S(1)}, u32[]{:S(2)}, u32[]{:S(2)}) collective-permute-start(bf16[1040,128]{1,0:T(8,128)(2,1)S(1)} %shard_map.100.refs_0_), channel_id=1, source_target_pairs={{0,16},{1,17},{2,18},{3,19},{4,20},{5,21},{6,22},{7,23},{8,24},{9,... | collective-permute-start | bytes 798728 | tf_op jit(solution)/shard_map/ppermute | solution.py:40
  7.3 6.0 %collective-permute-start.1 = (bf16[128,1024]{1,0:T(8,128)(2,1)}, bf16[128,1024]{1,0:T(8,128)(2,1)S(1)}, u32[]{:S(2)}, u32[]{:S(2)}) collective-permute-start(bf16[128,1024]{1,0:T(8,128)(2,1)} %refs_2_.4), channel_id=1, source_target_pairs={{0,32},{1,97},{2,34},{3,99},{4,36},{5,101},{6,38},{7,103},{8,40},{... | collective-permute-start | bytes 786440 | tf_op jit(solution)/shard_map/ppermute | solution.py:40
  10.2 10.0 %collective-permute-start.8 = (bf16[1040,128]{1,0:T(8,128)(2,1)S(1)}, bf16[1040,128]{1,0:T(8,128)(2,1)S(1)}, u32[]{:S(2)}, u32[]{:S(2)}) collective-permute-start(bf16[1040,128]{1,0:T(8,128)(2,1)S(1)} %shard_map.100.refs_0_), channel_id=1, source_target_pairs={{0,128},{1,145},{2,130},{3,147},{4,132},{5,149},{6,134},{7,151},{8... | collective-permute-start | bytes 798728 | tf_op jit(solution)/shard_map/ppermute | solution.py:40
  11.0 4.4 %collective-permute-start.2 = (bf16[128,1024]{1,0:T(8,128)(2,1)S(1)}, bf16[128,1024]{1,0:T(8,128)(2,1)S(1)}, u32[]{:S(2)}, u32[]{:S(2)}) collective-permute-start(bf16[128,1024]{1,0:T(8,128)(2,1)S(1)} %collective-permute-done.refs_3_), channel_id=1, source_target_pairs={{0,1},{1,0},{2,3},{3,2},{4,5},{5,4},{6,7},{7,6},{8,9},{9,8},{10,11... | collective-permute-start | bytes 786440 | tf_op jit(solution)/shard_map/ppermute | solution.py:40
  11.8 7.7 %collective-permute-start.4 = (bf16[128,1024]{1,0:T(8,128)(2,1)S(1)}, bf16[128,1024]{1,0:T(8,128)(2,1)S(1)}, u32[]{:S(2)}, u32[]{:S(2)}) collective-permute-start(bf16[128,1024]{1,0:T(8,128)(2,1)S(1)} %collective-permute-done.refs_3_), channel_id=1, source_target_pairs={{0,32},{1,97},{2,34},{3,99},{4,36},{5,101},{6,38},{7,103},{8,40},{... | collective-permute-start | bytes 786440 | tf_op jit(solution)/shard_map/ppermute | solution.py:40
  13.3 6.9 %collective-permute-start.5 = (bf16[128,1024]{1,0:T(8,128)(2,1)S(1)}, bf16[128,1024]{1,0:T(8,128)(2,1)S(1)}, u32[]{:S(2)}, u32[]{:S(2)}) collective-permute-start(bf16[128,1024]{1,0:T(8,128)(2,1)S(1)} %collective-permute-done.1.refs_4_), channel_id=1, source_target_pairs={{0,32},{1,97},{2,34},{3,99},{4,36},{5,101},{6,38},{7,103},{8,40},{... | collective-permute-start | bytes 786440 | tf_op jit(solution)/shard_map/ppermute | solution.py:40
  14.8 5.3 %collective-permute-start.3 = (bf16[128,1024]{1,0:T(8,128)(2,1)S(1)}, bf16[128,1024]{1,0:T(8,128)(2,1)S(1)}, u32[]{:S(2)}, u32[]{:S(2)}) collective-permute-start(bf16[128,1024]{1,0:T(8,128)(2,1)S(1)} %collective-permute-done.1.refs_4_), channel_id=1, source_target_pairs={{0,1},{1,0},{2,3},{3,2},{4,5},{5,4},{6,7},{7,6},{8,9},{9,8},{10,11... | collective-permute-start | bytes 786440 | tf_op jit(solution)/shard_map/ppermute | solution.py:40
  15.4 4.8 %copy-start = (bf16[128,1024]{1,0:T(8,128)(2,1)S(1)}, bf16[128,1024]{1,0:T(8,128)(2,1)}, u32[]{:S(2)}) copy-start(bf16[128,1024]{1,0:T(8,128)(2,1)} %refs_1_.4) | copy-start | bytes 786436
  15.4 4.8 %copy-start.1 = (bf16[128,1024]{1,0:T(8,128)(2,1)S(1)}, bf16[128,1024]{1,0:T(8,128)(2,1)}, u32[]{:S(2)}) copy-start(bf16[128,1024]{1,0:T(8,128)(2,1)} %refs_2_.4) | copy-start | bytes 786436
  17.1 4.8 %copy-start.2 = (bf16[4,4,1024]{2,1,0:T(4,128)(2,1)S(1)}, bf16[4,4,1024]{2,1,0:T(4,128)(2,1)}, u32[]{:S(2)}) copy-start(bf16[4,4,1024]{2,1,0:T(4,128)(2,1)} %param.18) | copy-start | bytes 98308
  17.1 4.8 %copy-start.3 = (bf16[4,4,1024]{2,1,0:T(4,128)(2,1)S(1)}, bf16[4,4,1024]{2,1,0:T(4,128)(2,1)}, u32[]{:S(2)}) copy-start(bf16[4,4,1024]{2,1,0:T(4,128)(2,1)} %param.19) | copy-start | bytes 98308
  17.1 9.7 %collective-permute-start.7 = (bf16[1056,128]{1,0:T(8,128)(2,1)S(1)}, bf16[1056,128]{1,0:T(8,128)(2,1)S(1)}, u32[]{:S(2)}, u32[]{:S(2)}) collective-permute-start(bf16[1056,128]{1,0:T(8,128)(2,1)S(1)} %shard_map.103), channel_id=1, source_target_pairs={{0,16},{1,17},{2,18},{3,19},{4,20},{5,21},{6,22},{7,23},{8,24},{9,... | collective-permute-start | bytes 811016 | tf_op jit(solution)/shard_map/ppermute | solution.py:40
  21.5 8.3 %collective-permute-start.9 = (bf16[1056,128]{1,0:T(8,128)(2,1)S(1)}, bf16[1056,128]{1,0:T(8,128)(2,1)S(1)}, u32[]{:S(2)}, u32[]{:S(2)}) collective-permute-start(bf16[1056,128]{1,0:T(8,128)(2,1)S(1)} %shard_map.105), channel_id=1, source_target_pairs={{0,144},{1,129},{2,146},{3,131},{4,148},{5,133},{6,150},{7,135},{8... | collective-permute-start | bytes 811016 | tf_op jit(solution)/shard_map/ppermute | solution.py:40
